TPU v7x, 512 devices: a whole 4x4x16 slice. The times are simulated.
512 devices in a mesh: chan: 64 (over z_lo, x, core), freq: 8 (over y, z_hi).
Axes of the slice: x: 4, y: 4, z: 16 (z_hi: 2, z_lo: 8; z = z_hi * 8 + z_lo), core: 2. Of those that a mesh axis runs over, the one named last changes fastest.
Arguments:
- spectra: bfloat16 [20, 272, 2, 8192], P(None, 'freq', None, 'chan'), may hold values from -18 to 18
- valid: int32 [20, 8192], P(None, 'chan'), may hold values from 0 to 1
Outputs:
- correlation: float32 [4, 64, 51, 128, 128], P(None, 'chan', None, 'freq')
All inputs are finite; a program needn't handle non-finite values.
Results may differ from a plain program's by a relative error of at most 0.0045.
Values may be sent and summed in bfloat16 or wider, within the bound.
A program may use at most 64 MiB of HBM per device.

v0:
```python
import math

import jax
import jax.numpy as jnp
from jax import lax
from jax.sharding import PartitionSpec as P

BINS = 272
LAGS = 51
ROUNDS = 4
SMOOTH = 4


water_level = 0.5
first_bin = 30.0
period = 600.0


def extended(block, sides, width):
    for axis, dim in sides:
        count = lax.axis_size(axis)
        forward = [(i, i + 1) for i in range(count - 1)]
        backward = [(target, source) for source, target in forward]
        low = lax.ppermute(
            lax.slice_in_dim(block, block.shape[dim] - width, None, axis=dim), axis, forward
        )
        high = lax.ppermute(lax.slice_in_dim(block, 0, width, axis=dim), axis, backward)
        block = jnp.concatenate([low, block, high], axis=dim)
    return block


def from_behind(block, axis, distance):
    devices = range(lax.axis_size(axis))
    route = [((i - distance) % len(devices), i) for i in devices]
    return lax.ppermute(block, axis, route)


def make_table():
    lag_index = jnp.arange(LAGS, dtype=jnp.float32) - float(LAGS // 2)
    bin_freq = first_bin + jnp.arange(BINS, dtype=jnp.float32)
    phase_angle = 2.0 * math.pi * lag_index[:, None] * bin_freq[None, :] / period
    return jnp.concatenate([jnp.cos(phase_angle), -jnp.sin(phase_angle)], axis=1).astype(
        jnp.bfloat16
    )


def cross_spectrum(own_block, own_flags, partner_block, partner_flags):
    rotated = jnp.stack([partner_block[:, :, 1], -partner_block[:, :, 0]], axis=2)
    both_parts = jnp.concatenate([partner_block, rotated], axis=3)
    cross = lax.dot_general(
        own_block, both_parts, (((0, 2), (0, 2)), ((1,), (1,))), preferred_element_type=jnp.float32
    )
    pairs = lax.dot_general(
        own_flags, partner_flags, (((0,), (0,)), ((), ())), preferred_element_type=jnp.float32
    )
    divisor = jnp.maximum(jnp.concatenate([pairs, pairs], axis=1), 1.0)
    return (cross / divisor[None]).astype(jnp.bfloat16)


def lag_each(pieces):
    real_part, imag_part = pieces
    combined = jnp.concatenate([real_part, imag_part], axis=0)
    rows_here = combined.shape[1]
    cols_here = combined.shape[2]
    lag_values = jnp.dot(
        make_table(),
        combined.reshape(2 * BINS, rows_here * cols_here),
        preferred_element_type=jnp.float32,
    )
    return lag_values.reshape(LAGS, rows_here, cols_here)


def on_device(spectra, valid):
    block_width = spectra.shape[3]
    bin_dev = spectra.shape[1]
    padded = extended(spectra, (("freq", 1),), SMOOTH)
    values_pad = padded.astype(jnp.float32)
    magnitude = jnp.sqrt(
        values_pad[:, :, 0] * values_pad[:, :, 0] + values_pad[:, :, 1] * values_pad[:, :, 1]
    )
    running_sum = magnitude[:, 0:bin_dev]
    for offset in range(1, 2 * SMOOTH + 1):
        running_sum = running_sum + magnitude[:, offset : offset + bin_dev]
    bin_index = lax.axis_index("freq") * bin_dev + jnp.arange(bin_dev, dtype=jnp.int32)
    bin_count = (
        jnp.minimum(bin_index + SMOOTH, BINS - 1) - jnp.maximum(bin_index - SMOOTH, 0) + 1
    ).astype(jnp.float32)
    water_mark = jnp.maximum(running_sum / bin_count[None, :, None], water_level)
    factor = valid.astype(jnp.float32)[:, None, :] / water_mark
    whitened = (spectra.astype(jnp.float32) * factor[:, :, None, :]).astype(jnp.bfloat16)
    own_flags = valid.astype(jnp.bfloat16)
    partner_block = whitened
    partner_flags = own_flags
    spectra_list = []
    for round_index in range(ROUNDS):
        if round_index > 0:
            partner_block, partner_flags = from_behind((whitened, own_flags), "chan", round_index)
        spectra_list.append(cross_spectrum(whitened, own_flags, partner_block, partner_flags))
    results = []
    for spectrum in spectra_list:
        real_part = spectrum[:, :, :block_width]
        imag_part = spectrum[:, :, block_width:]
        results.append(
            lag_each(
                (
                    lax.all_to_all(real_part, "freq", split_axis=1, concat_axis=0, tiled=True),
                    lax.all_to_all(imag_part, "freq", split_axis=1, concat_axis=0, tiled=True),
                )
            )
        )
    correlation = jnp.stack(results, axis=0)
    return correlation[:, None]


def solution(mesh):
    return jax.shard_map(
        on_device,
        mesh=mesh,
        in_specs=(P(None, "freq", None, "chan"), P(None, "chan")),
        out_specs=P(None, "chan", None, "freq", None),
        check_vma=False,
    )
```

profile of v0, /device:TPU:102, one launch (start us, length us, event | category | flops | bytes accessed | tf_op | source)
XLA Modules:
  0.0 594.3 jit_solution(15846580449182252383)
XLA Ops:
  0.0 1.0 copy.33
  1.1 13.0 %collective-permute-start = (bf16[20,4,2,128]{3,1,0,2:T(4,128)(2,1)S(1)}, bf16[20,4,2,128]{3,1,0,2:T(4,128)(2,1)S(1)}, u32[]{:S(2)}, u32[]{:S(2)}) collective-permute-start(bf16[20,4,2,128]{3,1,0,2:T(4,128)(2,1)S(1)} %get-tuple-element.21), channel_id=1, source_target_pairs={{0,1},{1,2},{2,3},{3,4},{4,5},{5,6},{6,7},{8,9},{9,10},{10,11},{11... | collective-permute-start | bytes 122888 | tf_op jit(solution)/shard_map/ppermute | solution.py:24
  14.1 1.3 collective-permute-start.1
  15.4 0.8 fusion.67
  16.6 12.2 %collective-permute-done.1 = bf16[20,4,2,128]{3,1,0,2:T(4,128)(2,1)S(1)} collective-permute-done((bf16[20,4,2,128]{3,1,0,2:T(4,128)(2,1)S(1)}, bf16[20,4,2,128]{3,1,0,2:T(4,128)(2,1)S(1)}, u32[]{:S(2)}, u32[]{:S(2)}) %collective-permute-start.1) | collective-permute-done | bytes 40992 | tf_op jit(solution)/shard_map/ppermute | solution.py:27
  29.6 0.5 copy-done.2
  30.3 0.8 fusion.3
  31.1 0.6 fusion.58
  31.7 1.9 copy.38
  33.6 5.3 all-to-all-start
  38.9 1.8 copy.40
  40.7 100.9 %all-to-all-done = bf16[34,128,128]{2,0,1:T(8,128)(2,1)S(1)} async-done(((bf16[34,128,128]{2,0,1:T(8,128)(2,1)}), bf16[34,128,128]{2,0,1:T(8,128)(2,1)S(1)}, u32[]{:S(2)}, u32[]{:S(2)}) %all-to-all-start) | async-done | bytes 1114144 | tf_op jit(solution)/shard_map/all_to_all | solution.py:106
  141.6 3.6 all-to-all-start.1
  145.1 1.9 collective-permute-start.2
  147.1 1.9 collective-permute-start.3
  149.0 5.6 collective-permute-done.3
  155.0 1.1 fusion.63
  156.0 1.8 fusion.2
  157.9 1.4 fusion.59
  159.3 1.8 copy.44
  161.1 48.2 %all-to-all-done.1 = bf16[34,128,128]{2,0,1:T(8,128)(2,1)S(1)} async-done(((bf16[34,128,128]{2,0,1:T(8,128)(2,1)}), bf16[34,128,128]{2,0,1:T(8,128)(2,1)S(1)}, u32[]{:S(2)}, u32[]{:S(2)}) %all-to-all-start.1) | async-done | bytes 1114144 | tf_op jit(solution)/shard_map/all_to_all | solution.py:107
  209.3 12.5 %all-to-all-start.2 = ((bf16[34,128,128]{2,0,1:T(8,128)(2,1)}), bf16[34,128,128]{2,0,1:T(8,128)(2,1)}, u32[]{:S(2)}, u32[]{:S(2)}) async-start(bf16[34,128,128]{2,0,1:T(8,128)(2,1)} %copy.44), calls=%async_computation.2 | async-start | bytes 2621440 | tf_op jit(solution)/shard_map/all_to_all | solution.py:106
  221.8 3.0 copy.46
  224.8 42.1 %all-to-all-done.2 = bf16[34,128,128]{2,0,1:T(8,128)(2,1)} async-done(((bf16[34,128,128]{2,0,1:T(8,128)(2,1)}), bf16[34,128,128]{2,0,1:T(8,128)(2,1)}, u32[]{:S(2)}, u32[]{:S(2)}) %all-to-all-start.2) | async-done | bytes 1114144 | tf_op jit(solution)/shard_map/all_to_all | solution.py:106
  266.9 7.8 %all-to-all-start.3 = ((bf16[34,128,128]{2,0,1:T(8,128)(2,1)}), bf16[34,128,128]{2,0,1:T(8,128)(2,1)}, u32[]{:S(2)}, u32[]{:S(2)}) async-start(bf16[34,128,128]{2,0,1:T(8,128)(2,1)} %copy.46), calls=%async_computation.3 | async-start | bytes 2621440 | tf_op jit(solution)/shard_map/all_to_all | solution.py:107
  274.7 1.9 collective-permute-start.4
  276.6 2.2 collective-permute-start.5
  278.8 78.7 %collective-permute-done.5 = bf16[20,128]{1,0:T(8,128)(2,1)S(1)} collective-permute-done((bf16[20,128]{1,0:T(8,128)(2,1)S(1)}, bf16[20,128]{1,0:T(8,128)(2,1)S(1)}, u32[]{:S(2)}, u32[]{:S(2)}) %collective-permute-start.5) | collective-permute-done | bytes 5152 | tf_op jit(solution)/shard_map/ppermute | solution.py:35
  357.8 1.1 fusion.64
  358.9 1.8 fusion.1
  360.7 1.4 fusion.60
  362.2 1.9 copy.50
  364.0 14.4 %all-to-all-start.4 = ((bf16[34,128,128]{2,0,1:T(8,128)(2,1)}), bf16[34,128,128]{2,0,1:T(8,128)(2,1)}, u32[]{:S(2)}, u32[]{:S(2)}) async-start(bf16[34,128,128]{2,0,1:T(8,128)(2,1)} %copy.50), calls=%async_computation.4 | async-start | bytes 2621440 | tf_op jit(solution)/shard_map/all_to_all | solution.py:106
  378.4 3.0 copy.52
  381.5 41.3 %all-to-all-done.4 = bf16[34,128,128]{2,0,1:T(8,128)(2,1)} async-done(((bf16[34,128,128]{2,0,1:T(8,128)(2,1)}), bf16[34,128,128]{2,0,1:T(8,128)(2,1)}, u32[]{:S(2)}, u32[]{:S(2)}) %all-to-all-start.4) | async-done | bytes 1114144 | tf_op jit(solution)/shard_map/all_to_all | solution.py:106
  422.8 18.7 %all-to-all-start.5 = ((bf16[34,128,128]{2,0,1:T(8,128)(2,1)}), bf16[34,128,128]{2,0,1:T(8,128)(2,1)}, u32[]{:S(2)}, u32[]{:S(2)}) async-start(bf16[34,128,128]{2,0,1:T(8,128)(2,1)} %copy.52), calls=%async_computation.5 | async-start | bytes 2621440 | tf_op jit(solution)/shard_map/all_to_all | solution.py:107
  441.5 1.9 collective-permute-start.6
  443.5 2.1 collective-permute-start.7
  445.6 9.0 %collective-permute-done.7 = bf16[20,128]{1,0:T(8,128)(2,1)S(1)} collective-permute-done((bf16[20,128]{1,0:T(8,128)(2,1)S(1)}, bf16[20,128]{1,0:T(8,128)(2,1)S(1)}, u32[]{:S(2)}, u32[]{:S(2)}) %collective-permute-start.7) | collective-permute-done | bytes 5152 | tf_op jit(solution)/shard_map/ppermute | solution.py:35
  454.9 1.1 fusion.65
  456.0 1.8 fusion
  457.8 1.5 fusion.61
  459.3 1.9 copy.56
  461.1 25.1 %all-to-all-done.5 = bf16[34,128,128]{2,0,1:T(8,128)(2,1)} async-done(((bf16[34,128,128]{2,0,1:T(8,128)(2,1)}), bf16[34,128,128]{2,0,1:T(8,128)(2,1)}, u32[]{:S(2)}, u32[]{:S(2)}) %all-to-all-start.5) | async-done | bytes 1114144 | tf_op jit(solution)/shard_map/all_to_all | solution.py:107
  486.2 33.3 %all-to-all-start.6 = ((bf16[34,128,128]{2,0,1:T(8,128)(2,1)}), bf16[34,128,128]{2,0,1:T(8,128)(2,1)}, u32[]{:S(2)}, u32[]{:S(2)}) async-start(bf16[34,128,128]{2,0,1:T(8,128)(2,1)} %copy.56), calls=%async_computation.6 | async-start | bytes 2621440 | tf_op jit(solution)/shard_map/all_to_all | solution.py:106
  519.5 3.0 copy.58
  522.6 25.7 %all-to-all-done.6 = bf16[34,128,128]{2,0,1:T(8,128)(2,1)} async-done(((bf16[34,128,128]{2,0,1:T(8,128)(2,1)}), bf16[34,128,128]{2,0,1:T(8,128)(2,1)}, u32[]{:S(2)}, u32[]{:S(2)}) %all-to-all-start.6) | async-done | bytes 1114144 | tf_op jit(solution)/shard_map/all_to_all | solution.py:106
  548.3 16.7 %all-to-all-start.7 = ((bf16[34,128,128]{2,0,1:T(8,128)(2,1)}), bf16[34,128,128]{2,0,1:T(8,128)(2,1)}, u32[]{:S(2)}, u32[]{:S(2)}) async-start(bf16[34,128,128]{2,0,1:T(8,128)(2,1)} %copy.58), calls=%async_computation.7 | async-start | bytes 2621440 | tf_op jit(solution)/shard_map/all_to_all | solution.py:107
  565.7 0.5 copy_bitcast_fusion.6
  566.3 1.3 fusion.16
  567.6 2.5 copy.45
  570.1 2.5 copy.47
  572.6 1.5 copy.51
  574.1 1.5 copy.53
  575.6 1.5 copy.57
  577.0 9.7 %all-to-all-done.7 = bf16[34,128,128]{2,0,1:T(8,128)(2,1)} async-done(((bf16[34,128,128]{2,0,1:T(8,128)(2,1)}), bf16[34,128,128]{2,0,1:T(8,128)(2,1)}, u32[]{:S(2)}, u32[]{:S(2)}) %all-to-all-start.7) | async-done | bytes 1114144 | tf_op jit(solution)/shard_map/all_to_all | solution.py:107
  586.7 1.6 copy.59
  588.7 0.5 copy_bitcast_fusion.4
  589.5 0.6 fusion.19
  590.0 0.5 copy_bitcast_fusion.2
  590.6 0.6 fusion.22
  591.1 0.5 copy_bitcast_fusion
  591.7 0.6 fusion.25
  592.8 1.5 copy.61
  (46 shorter events, 4.2 us)
Async XLA Ops:
  1.1 15.5 %collective-permute-start = (bf16[20,4,2,128]{3,1,0,2:T(4,128)(2,1)S(1)}, bf16[20,4,2,128]{3,1,0,2:T(4,128)(2,1)S(1)}, u32[]{:S(2)}, u32[]{:S(2)}) collective-permute-start(bf16[20,4,2,128]{3,1,0,2:T(4,128)(2,1)S(1)} %get-tuple-element.21), channel_id=1, source_target_pairs={{0,1},{1,2},{2,3},{3,4},{4,5},{5,6},{6,7},{8,9},{9,10},{10,11},{11... | collective-permute-start | bytes 122888 | tf_op jit(solution)/shard_map/ppermute | solution.py:24
  14.1 14.6 %collective-permute-start.1 = (bf16[20,4,2,128]{3,1,0,2:T(4,128)(2,1)S(1)}, bf16[20,4,2,128]{3,1,0,2:T(4,128)(2,1)S(1)}, u32[]{:S(2)}, u32[]{:S(2)}) collective-permute-start(bf16[20,4,2,128]{3,1,0,2:T(4,128)(2,1)S(1)} %get-tuple-element.22), channel_id=1, source_target_pairs={{1,0},{2,1},{3,2},{4,3},{5,4},{6,5},{7,6},{9,8},{10,9},{11,10},{12... | collective-permute-start | bytes 122888 | tf_op jit(solution)/shard_map/ppermute | solution.py:27
  29.1 1.0 copy-start.2
  33.6 108.0 %all-to-all-start = ((bf16[34,128,128]{2,0,1:T(8,128)(2,1)}), bf16[34,128,128]{2,0,1:T(8,128)(2,1)S(1)}, u32[]{:S(2)}, u32[]{:S(2)}) async-start(bf16[34,128,128]{2,0,1:T(8,128)(2,1)} %copy.38), calls=%async_computation | async-start | bytes 2621440 | tf_op jit(solution)/shard_map/all_to_all | solution.py:106
  141.6 67.8 %all-to-all-start.1 = ((bf16[34,128,128]{2,0,1:T(8,128)(2,1)}), bf16[34,128,128]{2,0,1:T(8,128)(2,1)S(1)}, u32[]{:S(2)}, u32[]{:S(2)}) async-start(bf16[34,128,128]{2,0,1:T(8,128)(2,1)} %copy.40), calls=%async_computation.1 | async-start | bytes 2621440 | tf_op jit(solution)/shard_map/all_to_all | solution.py:107
  145.1 9.8 %collective-permute-start.2 = (bf16[20,34,2,128]{3,0,2,1:T(8,128)(2,1)S(1)}, bf16[20,34,2,128]{3,0,2,1:T(8,128)(2,1)}, u32[]{:S(2)}, u32[]{:S(2)}) collective-permute-start(bf16[20,34,2,128]{3,0,2,1:T(8,128)(2,1)S(1)} %multiply_convert_fusion), channel_id=1, source_target_pairs={{504,0},{0,8},{8,16},{16,24},{24,32},{32,40},{40,48},{48,56},{56,6... | collective-permute-start | bytes 1044488 | tf_op jit(solution)/shard_map/ppermute | solution.py:35
  147.1 7.5 %collective-permute-start.3 = (bf16[20,128]{1,0:T(8,128)(2,1)S(1)}, bf16[20,128]{1,0:T(8,128)(2,1)S(1)}, u32[]{:S(2)}, u32[]{:S(2)}) collective-permute-start(bf16[20,128]{1,0:T(8,128)(2,1)S(1)} %get-tuple-element.24), channel_id=1, source_target_pairs={{504,0},{0,8},{8,16},{16,24},{24,32},{32,40},{40,48},{48,56},{56,6... | collective-permute-start | bytes 15368 | tf_op jit(solution)/shard_map/ppermute | solution.py:35
  209.3 57.6 %all-to-all-start.2 = ((bf16[34,128,128]{2,0,1:T(8,128)(2,1)}), bf16[34,128,128]{2,0,1:T(8,128)(2,1)}, u32[]{:S(2)}, u32[]{:S(2)}) async-start(bf16[34,128,128]{2,0,1:T(8,128)(2,1)} %copy.44), calls=%async_computation.2 | async-start | bytes 2621440 | tf_op jit(solution)/shard_map/all_to_all | solution.py:106
  266.9 97.1 %all-to-all-start.3 = ((bf16[34,128,128]{2,0,1:T(8,128)(2,1)}), bf16[34,128,128]{2,0,1:T(8,128)(2,1)}, u32[]{:S(2)}, u32[]{:S(2)}) async-start(bf16[34,128,128]{2,0,1:T(8,128)(2,1)} %copy.46), calls=%async_computation.3 | async-start | bytes 2621440 | tf_op jit(solution)/shard_map/all_to_all | solution.py:107
  274.7 83.1 %collective-permute-start.4 = (bf16[20,34,2,128]{3,0,2,1:T(8,128)(2,1)S(1)}, bf16[20,34,2,128]{3,0,2,1:T(8,128)(2,1)}, u32[]{:S(2)}, u32[]{:S(2)}) collective-permute-start(bf16[20,34,2,128]{3,0,2,1:T(8,128)(2,1)S(1)} %multiply_convert_fusion), channel_id=1, source_target_pairs={{496,0},{504,8},{0,16},{8,24},{16,32},{24,40},{32,48},{40,56},{48,... | collective-permute-start | bytes 1044488 | tf_op jit(solution)/shard_map/ppermute | solution.py:35
  276.6 80.9 %collective-permute-start.5 = (bf16[20,128]{1,0:T(8,128)(2,1)S(1)}, bf16[20,128]{1,0:T(8,128)(2,1)S(1)}, u32[]{:S(2)}, u32[]{:S(2)}) collective-permute-start(bf16[20,128]{1,0:T(8,128)(2,1)S(1)} %get-tuple-element.24), channel_id=1, source_target_pairs={{496,0},{504,8},{0,16},{8,24},{16,32},{24,40},{32,48},{40,56},{48,... | collective-permute-start | bytes 15368 | tf_op jit(solution)/shard_map/ppermute | solution.py:35
  364.0 58.8 %all-to-all-start.4 = ((bf16[34,128,128]{2,0,1:T(8,128)(2,1)}), bf16[34,128,128]{2,0,1:T(8,128)(2,1)}, u32[]{:S(2)}, u32[]{:S(2)}) async-start(bf16[34,128,128]{2,0,1:T(8,128)(2,1)} %copy.50), calls=%async_computation.4 | async-start | bytes 2621440 | tf_op jit(solution)/shard_map/all_to_all | solution.py:106
  422.8 63.4 %all-to-all-start.5 = ((bf16[34,128,128]{2,0,1:T(8,128)(2,1)}), bf16[34,128,128]{2,0,1:T(8,128)(2,1)}, u32[]{:S(2)}, u32[]{:S(2)}) async-start(bf16[34,128,128]{2,0,1:T(8,128)(2,1)} %copy.52), calls=%async_computation.5 | async-start | bytes 2621440 | tf_op jit(solution)/shard_map/all_to_all | solution.py:107
  441.5 13.3 %collective-permute-start.6 = (bf16[20,34,2,128]{3,0,2,1:T(8,128)(2,1)S(1)}, bf16[20,34,2,128]{3,0,2,1:T(8,128)(2,1)}, u32[]{:S(2)}, u32[]{:S(2)}) collective-permute-start(bf16[20,34,2,128]{3,0,2,1:T(8,128)(2,1)S(1)} %multiply_convert_fusion), channel_id=1, source_target_pairs={{488,0},{496,8},{504,16},{0,24},{8,32},{16,40},{24,48},{32,56},{40... | collective-permute-start | bytes 1044488 | tf_op jit(solution)/shard_map/ppermute | solution.py:35
  443.5 11.1 %collective-permute-start.7 = (bf16[20,128]{1,0:T(8,128)(2,1)S(1)}, bf16[20,128]{1,0:T(8,128)(2,1)S(1)}, u32[]{:S(2)}, u32[]{:S(2)}) collective-permute-start(bf16[20,128]{1,0:T(8,128)(2,1)S(1)} %get-tuple-element.24), channel_id=1, source_target_pairs={{488,0},{496,8},{504,16},{0,24},{8,32},{16,40},{24,48},{32,56},{40... | collective-permute-start | bytes 15368 | tf_op jit(solution)/shard_map/ppermute | solution.py:35
  486.2 62.0 %all-to-all-start.6 = ((bf16[34,128,128]{2,0,1:T(8,128)(2,1)}), bf16[34,128,128]{2,0,1:T(8,128)(2,1)}, u32[]{:S(2)}, u32[]{:S(2)}) async-start(bf16[34,128,128]{2,0,1:T(8,128)(2,1)} %copy.56), calls=%async_computation.6 | async-start | bytes 2621440 | tf_op jit(solution)/shard_map/all_to_all | solution.py:106
  548.3 38.4 %all-to-all-start.7 = ((bf16[34,128,128]{2,0,1:T(8,128)(2,1)}), bf16[34,128,128]{2,0,1:T(8,128)(2,1)}, u32[]{:S(2)}, u32[]{:S(2)}) async-start(bf16[34,128,128]{2,0,1:T(8,128)(2,1)} %copy.58), calls=%async_computation.7 | async-start | bytes 2621440 | tf_op jit(solution)/shard_map/all_to_all | solution.py:107
  565.4 0.9 copy-start.4
  565.4 0.9 copy-start.6
  586.7 1.6 copy-start
  586.7 2.0 copy-start.1
  588.7 0.8 copy-start.5
  588.7 0.8 copy-start.7
  591.7 1.0 copy-start.3
where the time goes:
time: 596 us; the launch traced here: 594 us
  waiting for transfers between devices  399 us (67%)
  starting transfers between devices  138 us (23%)
  local copies, waits for them, and re-layouts  41.3 us (7%)
  matrix products  10.1 us (2%)
    all_to_all x4, waiting for transfers between devices, on_device(): lax.all_to_all(real_part, 'freq', split_axis=1, concat_axis=0, tiled=True)  210 us
    ppermute x6, waiting for transfers between devices, from_behind(): return lax.ppermute(block, axis, route)  93.3 us
    all_to_all x4, waiting for transfers between devices, on_device(): lax.all_to_all(imag_part, 'freq', split_axis=1, concat_axis=0, tiled=True)  83 us
    all_to_all x4, starting transfers between devices, on_device(): lax.all_to_all(real_part, 'freq', split_axis=1, concat_axis=0, tiled=True)  65.5 us
    all_to_all x4, starting transfers between devices, on_device(): lax.all_to_all(imag_part, 'freq', split_axis=1, concat_axis=0, tiled=True)  46.7 us
    ppermute x1, starting transfers between devices, extended(): lax.ppermute(lax.slice_in_dim(block, block.shape[dim] - width, None, axis...  13 us
    slice x8, local copies, waits for them, and re-layouts, on_device(): real_part = spectrum[:, :, :block_width]  12.3 us
    ppermute x1, waiting for transfers between devices, extended(): lax.ppermute(lax.slice_in_dim(block, 0, width, axis=dim), axis, backward)  12.2 us
  transfers between devices with their start and end apart: 16, of which 11 were waited for; matrix products, arithmetic and copies ran while one was open for 7% of the time, Pallas kernels for 0%

commit v1 on v0

v1 whole, which is shorter than its diff:
```python
import functools
import math

import jax
import jax.numpy as jnp
from jax import lax
from jax.experimental import pallas as pl
from jax.experimental.pallas import tpu as pltpu
from jax.sharding import PartitionSpec as P

W = 20
BINS = 272
CH = 128
LAGS = 51
ROUNDS = 4
SMOOTH = 4
BLOCKS = 64

BAND = 34
GROUP = 68
ROWS = 2 * W
PAIR = 2 * ROWS
HALO = SMOOTH * ROWS
BAND_ROWS = BAND * ROWS
GROUP_ROWS = GROUP * ROWS
FLAG_ROWS = 48
STRIDE = 2 * GROUP
LAG_PAD = 56
OWN_ROWS = 16
HALF = 64
EDGES = ((0, 4), (30, 4))
MIDDLE = ((4, 12), (16, 10), (26, 4))
WHITEN = ((0, 6), (6, 5), (11, 6))

water_level = 0.5
first_bin = 30.0
period = 600.0
MESH = pl.DeviceIdType.MESH


def make_table():
    lag_index = jnp.arange(LAGS, dtype=jnp.float32) - float(LAGS // 2)
    bin_freq = first_bin + jnp.arange(BINS, dtype=jnp.float32)
    phase_angle = 2.0 * math.pi * lag_index[:, None] * bin_freq[None, :] / period
    return jnp.stack([jnp.cos(phase_angle), -jnp.sin(phase_angle)], axis=1).astype(jnp.bfloat16)


def roll4(x):
    return pltpu.roll(x, 4, axis=1)


def kernel(
    raw, flags, table, out,
    band, mag, white, lhs, inverse, spread, lagged, outbox, inbox,
    load_sem, z_send, z_recv, h_send, h_recv, f_send, f_recv, x_send, x_recv, y_send, y_recv,
):
    i, j = lax.axis_index("chan"), lax.axis_index("freq")
    y, zhi = j // 2, j % 2
    core = i % 2
    other = 1 - zhi

    def ahead(r):
        t = i + r + BLOCKS
        flip = (t // BLOCKS + 1) % 2
        return {"chan": t % BLOCKS, "freq": j + flip * (1 - 2 * zhi)}

    def along_y(d):
        return {"chan": i, "freq": ((y + d) % 4) * 2 + zhi}

    across = {"chan": i, "freq": j + 1 - 2 * zhi}
    own_at = HALO + zhi * BAND_ROWS
    other_at = HALO + other * BAND_ROWS

    def remote(src, dst, send, recv, device):
        return pltpu.make_async_remote_copy(
            src_ref=src, dst_ref=dst, send_sem=send, recv_sem=recv,
            device_id=device, device_id_type=MESH,
        )

    load = pltpu.make_async_copy(raw, band.at[pl.ds(own_at, BAND_ROWS)], load_sem)
    load.start()
    barrier = pltpu.get_barrier_semaphore()
    partners = [across] + [along_y(d) for d in (1, 2, 3)]
    partners += [ahead(r) for r in (1, 2, 3, -1, -2, -3)]
    for partner in partners:
        pl.semaphore_signal(barrier, inc=1, device_id=partner, device_id_type=MESH)
    white[0, 0:FLAG_ROWS, :] = flags[...].astype(jnp.bfloat16)
    load.wait()
    pl.semaphore_wait(barrier, len(partners))

    z_pieces = EDGES + MIDDLE

    def z_copy(k):
        first, bins = z_pieces[k]
        here = band.at[pl.ds(own_at + first * ROWS, bins * ROWS)]
        return remote(here, here, z_send.at[k], z_recv.at[k], across)

    for k in range(len(z_pieces)):
        z_copy(k).start()

    def halo_copy(top, k):
        src = HALO + GROUP_ROWS - HALO if top else HALO
        dst = 0 if top else HALO + GROUP_ROWS
        return remote(
            band.at[pl.ds(src, HALO)], band.at[pl.ds(dst, HALO)],
            h_send.at[k], h_recv.at[k], along_y(1 if top else 3),
        )

    @pl.when(zhi == 1)
    def _():
        halo_copy(True, 0).start()

    @pl.when(zhi == 0)
    def _():
        halo_copy(False, 1).start()

    flag_copies = [
        remote(
            white.at[0, pl.ds(0, FLAG_ROWS)], white.at[r, pl.ds(0, FLAG_ROWS)],
            f_send.at[r - 1], f_recv.at[r - 1], ahead(r),
        )
        for r in (1, 2, 3)
    ]
    for copy in flag_copies:
        copy.start()

    sublane = lax.broadcasted_iota(jnp.int32, (1, 8, CH), 1)
    lane = lax.broadcasted_iota(jnp.int32, (1, 8, CH), 2)
    sign = jnp.where(sublane < 4, -1.0, 1.0)
    first_half = (lane % 32) < 16
    valid = flags[0:ROWS, :].astype(jnp.float32)

    def magnitudes(row, pairs):
        def body(p, carry):
            at = pl.multiple_of(row + p * PAIR, 16)
            v = band[pl.ds(at, PAIR), :].astype(jnp.float32).reshape(10, 8, CH)
            square = v * v
            m = jnp.sqrt(square + roll4(square))
            mag[pl.ds(at, PAIR), :] = m.reshape(PAIR, CH)
            return carry

        lax.fori_loop(0, pairs, body, 0, unroll=2 if pairs % 2 == 0 else 1)

    def whiten(first_pair, pairs):
        def body(p, carry):
            pair = first_pair + p
            row = pl.multiple_of(pair * PAIR, 16)
            m = [mag[pl.ds(pl.multiple_of(row + t * ROWS, 8), ROWS), :] for t in range(10)]
            inner = ((m[1] + m[2]) + (m[3] + m[4])) + ((m[5] + m[6]) + (m[7] + m[8]))
            outs = []
            for t in range(2):
                bin_index = y * GROUP + 2 * pair + t
                count = (
                    jnp.minimum(bin_index + SMOOTH, BINS - 1) - jnp.maximum(bin_index - SMOOTH, 0) + 1
                ).astype(jnp.float32)
                total = inner + (m[0] if t == 0 else m[9])
                water = jnp.maximum(total / jnp.full((ROWS, CH), count, jnp.float32), water_level)
                outs.append(valid / water)
            factor = jnp.concatenate(outs, axis=0)
            v = band[pl.ds(pl.multiple_of(row + HALO, 16), PAIR), :].astype(jnp.float32)
            w = (v * factor).astype(jnp.bfloat16)
            white[0, pl.ds(pl.multiple_of(FLAG_ROWS + row, 16), PAIR), :] = w
            a1 = pltpu.roll(w.astype(jnp.float32).reshape(10, 8, CH), 112 * zhi, axis=2)
            a2 = pltpu.roll(roll4(a1) * sign, 16, axis=2)
            both = jnp.where(first_half, a1, a2).reshape(PAIR, CH)
            turned = jnp.transpose(both)
            column = lax.broadcasted_iota(jnp.int32, (CH, PAIR), 1)
            lhs[pair, 0:CH, 0:PAIR] = jnp.where(column < ROWS, turned, 0.0).astype(jnp.bfloat16)
            lhs[pair, CH : 2 * CH, 0:PAIR] = jnp.where(column < ROWS, 0.0, turned).astype(jnp.bfloat16)
            return carry

        lax.fori_loop(0, pairs, body, 0)

    def cross(r, first_pair, pairs):
        def body(p, carry):
            pair = first_pair + p
            rhs = white[r, pl.ds(pl.multiple_of(FLAG_ROWS + pair * PAIR, 16), PAIR), :]
            c = jnp.dot(lhs[pair, :, 0:PAIR], rhs, preferred_element_type=jnp.float32)
            for t in range(2):
                for g in range(4):
                    scale = inverse[r, g * 16 : (g + 1) * 16, :]
                    for part in range(2):
                        at = t * CH + g * 32 + part * 16
                        start = g * 16 * STRIDE + part * GROUP + 2 * pair + t
                        spread[pl.ds(start, 16, stride=STRIDE), :] = c[at : at + 16, :] * scale
            return carry

        lax.fori_loop(0, pairs, body, 0)

    def usable_pairs(r):
        mine = white[0, 0:FLAG_ROWS, :].astype(jnp.float32)
        mine = pltpu.roll(mine, 112 * zhi, axis=1)
        n = jnp.dot(
            jnp.transpose(mine).astype(jnp.bfloat16), white[r, 0:FLAG_ROWS, :],
            preferred_element_type=jnp.float32,
        )
        scale = 1.0 / jnp.maximum(n * 0.5, 1.0)
        for g in range(4):
            inverse[r, g * 16 : (g + 1) * 16, :] = scale[g * 32 : g * 32 + 16, :]

    def lags(r):
        tab = table[...]

        def body(p, carry):
            a = 2 * p
            s0 = spread[pl.ds(pl.multiple_of(a * STRIDE, 8), STRIDE), :].astype(jnp.bfloat16)
            s1 = spread[pl.ds(pl.multiple_of((a + 1) * STRIDE, 8), STRIDE), :].astype(jnp.bfloat16)
            both = jnp.concatenate([s0, s1], axis=1)
            c = jnp.dot(tab, both, preferred_element_type=jnp.float32)
            lagged[r, pl.ds(a, LAG_PAD, stride=HALF), :] = c[:, 0:CH]
            lagged[r, pl.ds(a + 1, LAG_PAD, stride=HALF), :] = c[:, CH : 2 * CH]
            return carry

        lax.fori_loop(0, HALF // 2, body, 0)

        for d in (2, 1, 3):
            to = (y + d) % 4

            def pack(l, carry):
                at = pl.multiple_of(l * HALF + to * OWN_ROWS, 16)
                outbox[r, d - 1, pl.ds(pl.multiple_of(l * OWN_ROWS, 16), OWN_ROWS), :] = lagged[
                    r, pl.ds(at, OWN_ROWS), :
                ].astype(jnp.bfloat16)
                return carry

            lax.fori_loop(0, LAGS, pack, 0, unroll=3)
            y_copy(r, d).start()

    def y_copy(r, d):
        return remote(
            outbox.at[r, d - 1], inbox.at[r, d - 1], y_send.at[r, d - 1], y_recv.at[r, d - 1], along_y(d)
        )

    def piece(slot, k, origin):
        if k == 0:
            return white.at[slot, pl.ds(FLAG_ROWS + origin * BAND_ROWS, BAND_ROWS)]
        first, pairs = WHITEN[k - 1]
        return white.at[slot, pl.ds(FLAG_ROWS + (1 - origin) * BAND_ROWS + first * PAIR, pairs * PAIR)]

    x_index = (i // 2) % 4
    z_index = zhi * 8 + i // 8
    before = jnp.where(x_index == 0, ((z_index + 15) % 16) // 8, zhi)

    def to_sibling(k):
        return remote(piece(0, k, zhi), piece(1, k, zhi), x_send.at[0, k], x_recv.at[0, k], ahead(1))

    def to_next(k):
        return remote(piece(0, k, zhi), piece(2, k, zhi), x_send.at[1, k], x_recv.at[1, k], ahead(2))

    def pass_up(k):
        return remote(piece(2, k, before), piece(3, k, before), x_send.at[2, k], x_recv.at[2, k], ahead(1))

    def pass_down(k):
        return remote(piece(2, k, before), piece(1, k, before), x_send.at[2, k], x_recv.at[0, k], ahead(-1))

    def pass_on(k):
        return remote(piece(2, k, before), piece(3, k, before), x_send.at[0, k], x_recv.at[2, k], ahead(1))

    def send_own(k):
        to_next(k).start()

        @pl.when(core == 0)
        def _():
            to_sibling(k).start()

    def forward(k):
        to_next(k).wait_recv()

        @pl.when(core == 0)
        def _():
            pass_up(k).start()

        @pl.when(core == 1)
        def _():
            pass_down(k).start()
            pass_on(k).start()

    magnitudes(own_at, BAND // 2)
    usable_pairs(0)
    for k in range(len(EDGES)):
        z_copy(k).wait_recv()

    @pl.when(zhi == 0)
    def _():
        halo_copy(True, 0).start()

    @pl.when(zhi == 1)
    def _():
        halo_copy(False, 1).start()

    for first, bins in EDGES:
        magnitudes(other_at + first * ROWS, bins // 2)
    halo_copy(True, 0).wait_recv()
    halo_copy(False, 1).wait_recv()
    magnitudes(0, SMOOTH // 2)
    magnitudes(HALO + GROUP_ROWS, SMOOTH // 2)

    @pl.when(y == 0)
    def _():
        mag[0:HALO, :] = jnp.zeros((HALO, CH), jnp.float32)

    @pl.when(y == 3)
    def _():
        mag[HALO + GROUP_ROWS :, :] = jnp.zeros((HALO, CH), jnp.float32)

    whiten(zhi * (BAND // 2), BAND // 2)
    send_own(0)
    cross(0, zhi * (BAND // 2), BAND // 2)
    for k in (1, 2, 3):
        z_copy(1 + k).wait_recv()
        first, bins = MIDDLE[k - 1]
        magnitudes(other_at + first * ROWS, bins // 2)
        first, pairs = WHITEN[k - 1]
        whiten(other * (BAND // 2) + first, pairs)
        send_own(k)
        forward(k - 1)
        cross(0, other * (BAND // 2) + first, pairs)
    forward(3)
    lags(0)
    for r in (1, 2, 3):
        flag_copies[r - 1].wait_recv()
        usable_pairs(r)
        if r != 2:
            for k in range(4):
                remote(
                    piece(r, k, zhi), piece(r, k, zhi), x_send.at[0, k], x_recv.at[r - 1, k], ahead(1)
                ).wait_recv()
        cross(r, 0, GROUP // 2)
        lags(r)

    for r in range(ROUNDS):
        for d in (1, 2, 3):
            y_copy(r, d).wait_recv()

        def total(l, carry):
            at = pl.multiple_of(l * OWN_ROWS, 16)
            mine = lagged[r, pl.ds(pl.multiple_of(l * HALF + y * OWN_ROWS, 16), OWN_ROWS), :]
            got = [inbox[r, d, pl.ds(at, OWN_ROWS), :].astype(jnp.float32) for d in range(3)]
            out[r, pl.ds(at, OWN_ROWS), :] = (mine + got[0]) + (got[1] + got[2])
            return carry

        lax.fori_loop(0, LAGS, total, 0, unroll=3)

    for k in range(len(z_pieces)):
        z_copy(k).wait_send()
    halo_copy(True, 0).wait_send()
    halo_copy(False, 1).wait_send()
    for copy in flag_copies:
        copy.wait_send()
    for k in range(4):
        to_next(k).wait_send()
        to_sibling(k).wait_send()
        pass_up(k).wait_send()
    for r in range(ROUNDS):
        for d in (1, 2, 3):
            y_copy(r, d).wait_send()


def on_device(spectra, valid):
    groups = spectra.reshape(5, 4, BAND, 2, CH)
    raw = jnp.transpose(groups, (2, 0, 3, 1, 4)).reshape(BAND_ROWS, CH)
    flags = valid.astype(jnp.float32).reshape(5, 1, 4, CH)
    flags = jnp.broadcast_to(flags, (5, 2, 4, CH)).reshape(ROWS, CH)
    flags = jnp.pad(flags, ((0, FLAG_ROWS - ROWS), (0, 0)))
    y = lax.axis_index("freq") // 2
    table = lax.dynamic_slice_in_dim(make_table(), y * GROUP, GROUP, axis=2)
    table = jnp.pad(table.reshape(LAGS, STRIDE), ((0, LAG_PAD - LAGS), (0, 0)))
    vmem = pl.BlockSpec(memory_space=pltpu.VMEM)
    dma = pltpu.SemaphoreType.DMA
    bf16, f32 = jnp.bfloat16, jnp.float32
    out = pl.pallas_call(
        kernel,
        out_shape=jax.ShapeDtypeStruct((ROUNDS, LAGS * OWN_ROWS, CH), f32),
        in_specs=[pl.BlockSpec(memory_space=pl.ANY), vmem, vmem],
        out_specs=vmem,
        scratch_shapes=[
            pltpu.VMEM((GROUP_ROWS + 2 * HALO, CH), bf16),
            pltpu.VMEM((GROUP_ROWS + 2 * HALO, CH), f32),
            pltpu.VMEM((ROUNDS, FLAG_ROWS + GROUP_ROWS, CH), bf16),
            pltpu.VMEM((GROUP // 2, 2 * CH, CH), bf16),
            pltpu.VMEM((ROUNDS, HALF, CH), f32),
            pltpu.VMEM((HALF * STRIDE, CH), f32),
            pltpu.VMEM((ROUNDS, LAG_PAD * HALF, CH), f32),
            pltpu.VMEM((ROUNDS, 3, LAGS * OWN_ROWS, CH), bf16),
            pltpu.VMEM((ROUNDS, 3, LAGS * OWN_ROWS, CH), bf16),
            dma, dma((5,)), dma((5,)), dma((2,)), dma((2,)), dma((3,)), dma((3,)),
            dma((3, 4)), dma((3, 4)), dma((4, 3)), dma((4, 3)),
        ],
        compiler_params=pltpu.CompilerParams(
            collective_id=0, has_side_effects=True, vmem_limit_bytes=48 << 20
        ),
        name="correlate",
    )(raw, flags, table)
    return out.reshape(ROUNDS, 1, LAGS, OWN_ROWS, CH)


def solution(mesh):
    return jax.shard_map(
        on_device,
        mesh=mesh,
        in_specs=(P(None, "freq", None, "chan"), P(None, "chan")),
        out_specs=P(None, "chan", None, "freq", None),
        check_vma=False,
    )
```

time: 596 us -> 127 us (0.21)
  the two profiles are of different devices: /device:TPU:102 before, /device:TPU:3 now
where the time goes in v1:
time: 127 us; the launch traced here: 126 us
  Pallas kernels  120 us (94%)
  other arithmetic  3.49 us (3%)
  local copies, waits for them, and re-layouts  2.48 us (2%)
    pallas_call x1, Pallas kernels, on_device(): pl.pallas_call(kernel, out_shape=jax.ShapeDtypeStruct((ROUNDS, LAGS * OWN...  120 us
    another operation x1, other arithmetic  2.54 us

profile of v1, /device:TPU:3, one launch (start us, length us, event | category | flops | bytes accessed | tf_op | source)
XLA Modules:
  0.0 126.4 jit_solution(16925931419648813238)
XLA Ops:
  0.0 0.7 convert_element_type.8
  0.8 2.5 %negate_convert_fusion = (bf16[51,1,272]{2,1,0:T(2,128)(2,1)S(1)}, bf16[51,1,272]{2,1,0:T(2,128)(2,1)S(1)}) fusion(f32[272]{0:T(512)S(1)} %iota_add_fusion, f32[51]{0:T(128)S(1)} %add_multiply_fusion), kind=kLoop, calls=%fused_computation | loop fusion | flops 69360 | bytes 56780 | tf_op jit(solution)/shard_map/convert.1
  3.3 0.2 fusion
  3.5 0.1 reshape.117
  3.7 1.2 copy.3
  4.8 120.4 %correlate.1 = f32[4,816,128]{2,1,0:T(8,128)S(1)} custom-call(bf16[1360,128]{1,0:T(8,128)(2,1)S(1)} %bitcast.9, f32[48,128]{1,0:T(8,128)S(1)} %pad.8.flags, bf16[56,136]{1,0:T(8,128)(2,1)S(1)} %pad.9.table), custom_call_target="tpu_custom_call" | custom-call | tf_op jit(solution)/shard_map/correlate/pallas_call | solution.py:371
  125.2 1.2 copy.6
  (6 shorter events, 0.1 us)

commit v2 on v1

v2 whole, which is shorter than its diff:
```python
import math

import jax
import jax.numpy as jnp
import numpy as np
from jax import lax
from jax.experimental import pallas as pl
from jax.experimental.pallas import tpu as pltpu
from jax.sharding import PartitionSpec as P

W = 20
BINS = 272
CH = 128
LAGS = 51
ROUNDS = 4
SMOOTH = 4
BLOCKS = 64

BAND = 34
GROUP = 68
PAIRS = GROUP // 2
ROWS = 2 * W
PAIR = 2 * ROWS
HALO = SMOOTH * ROWS
BAND_ROWS = BAND * ROWS
GROUP_ROWS = GROUP * ROWS
FLAG_ROWS = 48
STRIDE = 2 * GROUP
LAG_STORE = 56
LAG_PAD = 64
OWN_ROWS = 16
HALF = 64
CUT = 26 * OWN_ROWS
FULL = LAGS * OWN_ROWS
ACROSS = ((0, 2), (12, 5), (8, 4), (4, 4), (2, 2))
WHITEN = ((2, 13), (0, 2), (15, 5), (20, 4), (24, 4), (28, 6))
PIECES = len(WHITEN)

water_level = 0.5
first_bin = 30.0
period = 600.0
MESH = pl.DeviceIdType.MESH


def make_table():
    lag_index = np.arange(LAGS, dtype=np.float32) - np.float32(LAGS // 2)
    bin_freq = np.float32(first_bin) + np.arange(BINS, dtype=np.float32)
    phase = np.float32(2.0 * math.pi) * lag_index[:, None] * bin_freq[None, :] / np.float32(period)
    both = np.stack([np.cos(phase), -np.sin(phase)], axis=1).reshape(LAGS, 2, 4, GROUP)
    table = np.zeros((4, LAG_PAD, 2, GROUP), np.float32)
    table[:, :LAGS] = both.transpose(2, 0, 1, 3)
    return jnp.asarray(table.reshape(4, LAG_PAD, STRIDE), jnp.bfloat16)


def roll4(x):
    return pltpu.roll(x, 4, axis=1)


def loop(count, body):
    lax.fori_loop(0, count, lambda n, carry: (body(n), carry)[1], 0, unroll=unrolled(count))


def unrolled(count):
    return max(n for n in range(1, 18) if count % n == 0)


def kernel(
    raw, flags, table, out,
    band, mag, white, lhs, inverse, spread, lagged, outbox, inbox,
    load_sem, z_send, z_recv, h_send, h_recv, f_send, f_recv, x_send, x_recv, y_send, y_recv,
):
    i, j = lax.axis_index("chan"), lax.axis_index("freq")
    y, zhi = j // 2, j % 2
    core = i % 2
    x_index = (i // 2) % 4
    z_index = zhi * 8 + i // 8
    before = jnp.where(x_index == 0, ((z_index + 15) % 16) // 8, zhi)

    def ahead(r):
        t = i + r + BLOCKS
        flip = (t // BLOCKS + 1) % 2
        return {"chan": t % BLOCKS, "freq": j + flip * (1 - 2 * zhi)}

    def along_y(d):
        return {"chan": i, "freq": ((y + d) % 4) * 2 + zhi}

    across = {"chan": i, "freq": j + 1 - 2 * zhi}

    def first_pair(first, pairs, origin):
        return first + origin * (PAIRS - 2 * first - pairs)

    def remote(src, dst, send, recv, device):
        return pltpu.make_async_remote_copy(
            src_ref=src, dst_ref=dst, send_sem=send, recv_sem=recv,
            device_id=device, device_id_type=MESH,
        )

    load = pltpu.make_async_copy(raw, band.at[pl.ds(HALO + zhi * BAND_ROWS, BAND_ROWS)], load_sem)
    load.start()
    barrier = pltpu.get_barrier_semaphore()
    partners = [across] + [along_y(d) for d in (1, 3)]
    partners += [ahead(r) for r in (1, 2, 3, -1, -2, -3)]
    for partner in partners:
        pl.semaphore_signal(barrier, inc=1, device_id=partner, device_id_type=MESH)
    white[0, 0:FLAG_ROWS, :] = flags[...].astype(jnp.bfloat16)
    load.wait()
    pl.semaphore_wait(barrier, len(partners))

    def z_copy(k):
        first, pairs = ACROSS[k]
        here = band.at[pl.ds(HALO + first_pair(first, pairs, zhi) * PAIR, pairs * PAIR)]
        return remote(here, here, z_send.at[k], z_recv.at[k], across)

    def halo_copy(top):
        src = GROUP_ROWS if top else HALO
        dst = 0 if top else HALO + GROUP_ROWS
        k = 0 if top else 1
        return remote(
            band.at[pl.ds(src, HALO)], band.at[pl.ds(dst, HALO)],
            h_send.at[k], h_recv.at[k], along_y(1 if top else 3),
        )

    def send_halo(own):
        pl.when(zhi == own)(halo_copy(True).start)
        pl.when(zhi != own)(halo_copy(False).start)

    flag_copies = [
        remote(
            white.at[0, pl.ds(0, FLAG_ROWS)], white.at[r, pl.ds(0, FLAG_ROWS)],
            f_send.at[r - 1], f_recv.at[r - 1], ahead(r),
        )
        for r in (1, 2, 3)
    ]

    sublane = lax.broadcasted_iota(jnp.int32, (1, 8, CH), 1)
    lane = lax.broadcasted_iota(jnp.int32, (1, 8, CH), 2)
    sign = jnp.where(sublane < 4, -1.0, 1.0)
    first_half = (lane % 32) < 16
    valid = flags[0:ROWS, :]

    def magnitudes(row, pairs):
        def body(p):
            at = pl.multiple_of(row + p * PAIR, 16)
            v = band[pl.ds(at, PAIR), :].astype(jnp.float32).reshape(10, 8, CH)
            square = v * v
            m = jnp.sqrt(square + roll4(square))
            mag[pl.ds(at, PAIR), :] = m.reshape(PAIR, CH)

        loop(pairs, body)

    def whiten(start, pairs):
        def body(p):
            pair = start + p
            row = pl.multiple_of(pair * PAIR, 16)
            m = [mag[pl.ds(pl.multiple_of(row + t * ROWS, 8), ROWS), :] for t in range(10)]
            inner = ((m[1] + m[2]) + (m[3] + m[4])) + ((m[5] + m[6]) + (m[7] + m[8]))
            outs = []
            for t in range(2):
                bin_index = y * GROUP + 2 * pair + t
                count = (
                    jnp.minimum(bin_index + SMOOTH, BINS - 1) - jnp.maximum(bin_index - SMOOTH, 0) + 1
                ).astype(jnp.float32)
                total = inner + (m[0] if t == 0 else m[9])
                water = jnp.maximum(total / jnp.full((1, CH), count, jnp.float32), water_level)
                outs.append(valid / water)
            factor = jnp.concatenate(outs, axis=0)
            v = band[pl.ds(pl.multiple_of(row + HALO, 16), PAIR), :].astype(jnp.float32)
            w = (v * factor).astype(jnp.bfloat16)
            white[0, pl.ds(pl.multiple_of(FLAG_ROWS + row, 16), PAIR), :] = w
            a1 = pltpu.roll(w.astype(jnp.float32).reshape(10, 8, CH), 112 * zhi, axis=2)
            a2 = pltpu.roll(roll4(a1) * sign, 16, axis=2)
            both = jnp.where(first_half, a1, a2).reshape(PAIR, CH)
            turned = jnp.transpose(both)
            column = lax.broadcasted_iota(jnp.int32, (CH, PAIR), 1)
            lhs[pair, 0:CH, 0:PAIR] = jnp.where(column < ROWS, turned, 0.0).astype(jnp.bfloat16)
            lhs[pair, CH : 2 * CH, 0:PAIR] = jnp.where(column < ROWS, 0.0, turned).astype(jnp.bfloat16)

        loop(pairs, body)

    def cross(r, start, pairs):
        def body(p):
            pair = start + p
            rhs = white[r, pl.ds(pl.multiple_of(FLAG_ROWS + pair * PAIR, 16), PAIR), :]
            c = jnp.dot(lhs[pair, :, 0:PAIR], rhs, preferred_element_type=jnp.float32)
            for g in range(4):
                scale = inverse[r, g * 16 : (g + 1) * 16, :]
                for t in range(2):
                    for part in range(2):
                        at = t * CH + g * 32 + part * 16
                        row = g * 16 * STRIDE + part * GROUP + 2 * pair + t
                        spread[pl.ds(row, 16, stride=STRIDE), :] = c[at : at + 16, :] * scale

        loop(pairs, body)

    def usable_pairs(r):
        mine = white[0, 0:FLAG_ROWS, :].astype(jnp.float32)
        mine = pltpu.roll(mine, 112 * zhi, axis=1)
        n = jnp.dot(
            jnp.transpose(mine).astype(jnp.bfloat16), white[r, 0:FLAG_ROWS, :],
            preferred_element_type=jnp.float32,
        )
        scale = 1.0 / jnp.maximum(n * 0.5, 1.0)
        for g in range(4):
            inverse[r, g * 16 : (g + 1) * 16, :] = scale[g * 32 : g * 32 + 16, :]

    def lag_sums(r):
        tab = table[y]

        def body(p):
            a = 2 * p
            s0 = spread[pl.ds(pl.multiple_of(a * STRIDE, 8), STRIDE), :].astype(jnp.bfloat16)
            s1 = spread[pl.ds(pl.multiple_of((a + 1) * STRIDE, 8), STRIDE), :].astype(jnp.bfloat16)
            both = jnp.concatenate([s0, s1], axis=1)
            c = jnp.dot(tab, both, preferred_element_type=jnp.float32)
            lagged[r, pl.ds(a, LAG_STORE, stride=HALF), :] = c[0:LAG_STORE, 0:CH]
            lagged[r, pl.ds(a + 1, LAG_STORE, stride=HALF), :] = c[0:LAG_STORE, CH : 2 * CH]

        loop(HALF // 2, body)

    PARTS = ((2, 0, 1), (2, CUT, 3), (1, CUT, 1), (3, 0, 3), (1, 0, 1), (3, CUT, 3))

    def y_copy(r, n):
        d, row, way = PARTS[n]
        part = pl.ds(row, CUT if row == 0 else FULL - CUT)
        return remote(
            outbox.at[r, d - 1, part], inbox.at[r, d - 1, part], y_send.at[r, n], y_recv.at[r, n], along_y(way)
        )

    def pack_round(r, n):
        d, row, _ = PARTS[n]
        to = (y + d) % 4

        def body(l):
            at = pl.multiple_of(row + l * OWN_ROWS, 16)
            from_row = pl.multiple_of(row // OWN_ROWS * HALF + l * HALF + to * OWN_ROWS, 16)
            sums = lagged[r, pl.ds(from_row, OWN_ROWS), :]
            if n >= 4:
                sums = sums + inbox[r, 1, pl.ds(at, OWN_ROWS), :].astype(jnp.float32)
            outbox[r, d - 1, pl.ds(at, OWN_ROWS), :] = sums.astype(jnp.bfloat16)

        loop((CUT if row == 0 else FULL - CUT) // OWN_ROWS, body)

    def lags(r):
        lag_sums(r)
        for n in range(4):
            pack_round(r, n)
            y_copy(r, n).start()

    def relay(r):
        for n in (0, 1):
            y_copy(r, n).wait_recv()
            pack_round(r, 4 + n)
            y_copy(r, 4 + n).start()

    def total_round(r):
        def body(l):
            at = pl.multiple_of(l * OWN_ROWS, 16)
            mine = lagged[r, pl.ds(pl.multiple_of(l * HALF + y * OWN_ROWS, 16), OWN_ROWS), :]
            got = [inbox[r, d, pl.ds(at, OWN_ROWS), :].astype(jnp.float32) for d in (0, 2)]
            out[r, pl.ds(at, OWN_ROWS), :] = mine + (got[0] + got[1])

        loop(LAGS, body)

    def finish(r):
        for n in (2, 3, 4, 5):
            y_copy(r, n).wait_recv()
        total_round(r)

    def piece(slot, k, origin):
        first, pairs = WHITEN[k]
        return white.at[slot, pl.ds(FLAG_ROWS + first_pair(first, pairs, origin) * PAIR, pairs * PAIR)]

    def to_sibling(k):
        return remote(piece(0, k, zhi), piece(1, k, zhi), x_send.at[0, k], x_recv.at[0, k], ahead(1))

    def to_next(k):
        return remote(piece(0, k, zhi), piece(2, k, zhi), x_send.at[1, k], x_recv.at[1, k], ahead(2))

    def pass_up(k):
        return remote(piece(2, k, before), piece(3, k, before), x_send.at[2, k], x_recv.at[2, k], ahead(1))

    def pass_down(k):
        return remote(piece(2, k, before), piece(1, k, before), x_send.at[2, k], x_recv.at[0, k], ahead(-1))

    def pass_on(k):
        return remote(piece(2, k, before), piece(3, k, before), x_send.at[0, k], x_recv.at[2, k], ahead(1))

    def send_own(k):
        pl.when(core == 0)(to_sibling(k).start)
        pl.when(x_index != 3)(to_next(k).start)

    def forward(k):
        to_next(k).wait_recv()
        pl.when(core == 0)(pass_up(k).start)
        pl.when(core == 1)(pass_down(k).start)
        pl.when((core == 1) & (x_index != 3))(pass_on(k).start)

    def forward_early(k):
        @pl.when(x_index != 0)
        def _():
            forward(k)

    def whiten_piece(k):
        first, pairs = WHITEN[k]
        whiten(first_pair(first, pairs, zhi), pairs)
        send_own(k)

    def cross_piece(k):
        first, pairs = WHITEN[k]
        cross(0, first_pair(first, pairs, zhi), pairs)

    def receive_across(k):
        z_copy(k).wait_recv()
        if k + 2 < len(ACROSS):
            z_copy(k + 2).start()
        if k == 0:
            send_halo(0)
        first, pairs = ACROSS[k]
        magnitudes(HALO + first_pair(first, pairs, 1 - zhi) * PAIR, pairs)

    z_copy(0).start()
    z_copy(1).start()
    send_halo(1)
    for copy in flag_copies:
        copy.start()
    magnitudes(HALO + zhi * BAND_ROWS, BAND // 2)
    whiten_piece(0)
    usable_pairs(0)
    receive_across(0)
    cross_piece(0)
    halo_copy(True).wait_recv()
    halo_copy(False).wait_recv()
    magnitudes(0, SMOOTH // 2)
    magnitudes(HALO + GROUP_ROWS, SMOOTH // 2)

    @pl.when(y == 0)
    def _():
        mag[0:HALO, :] = jnp.zeros((HALO, CH), jnp.float32)

    @pl.when(y == 3)
    def _():
        mag[HALO + GROUP_ROWS :, :] = jnp.zeros((HALO, CH), jnp.float32)

    whiten_piece(1)
    cross_piece(1)
    for k in range(2, PIECES):
        receive_across(k - 1)
        whiten_piece(k)
        forward_early(k - 2)
        if k < PIECES - 1:
            cross_piece(k)
        if k == 3:
            for r in (1, 2, 3):
                flag_copies[r - 1].wait_recv()
                usable_pairs(r)

    @pl.when(x_index == 3)
    def _():
        for k in range(PIECES):
            to_next(k).start()

    forward_early(PIECES - 2)
    cross_piece(PIECES - 1)
    lags(0)
    forward_early(PIECES - 1)

    @pl.when((x_index == 3) & (core == 1))
    def _():
        for k in range(PIECES):
            pass_on(k).start()

    @pl.when(x_index == 0)
    def _():
        for k in range(PIECES):
            forward(k)

    for r in (1, 2, 3):
        if r != 2:
            for k in range(PIECES):
                remote(
                    piece(r, k, zhi), piece(r, k, zhi), x_send.at[0, k], x_recv.at[r - 1, k], ahead(1)
                ).wait_recv()
        cross(r, 0, PAIRS)
        lags(r)
        relay(r - 1)
    finish(0)
    relay(3)
    for r in (1, 2, 3):
        finish(r)

    for k in range(len(ACROSS)):
        z_copy(k).wait_send()
    halo_copy(True).wait_send()
    halo_copy(False).wait_send()
    for copy in flag_copies:
        copy.wait_send()
    for k in range(PIECES):
        to_next(k).wait_send()
        to_sibling(k).wait_send()
        pass_up(k).wait_send()
    for r in range(ROUNDS):
        for n in range(len(PARTS)):
            y_copy(r, n).wait_send()


def on_device(spectra, valid):
    groups = spectra.reshape(5, 4, BAND, 2, CH)
    raw = jnp.transpose(groups, (2, 0, 3, 1, 4)).reshape(BAND_ROWS, CH)
    flags = valid.astype(jnp.float32).reshape(5, 1, 4, CH)
    flags = jnp.broadcast_to(flags, (5, 2, 4, CH)).reshape(ROWS, CH)
    flags = jnp.pad(flags, ((0, FLAG_ROWS - ROWS), (0, 0)))
    vmem = pl.BlockSpec(memory_space=pltpu.VMEM)
    dma = pltpu.SemaphoreType.DMA
    bf16, f32 = jnp.bfloat16, jnp.float32
    out = pl.pallas_call(
        kernel,
        out_shape=jax.ShapeDtypeStruct((ROUNDS, LAGS * OWN_ROWS, CH), f32),
        in_specs=[pl.BlockSpec(memory_space=pl.ANY), vmem, vmem],
        out_specs=vmem,
        scratch_shapes=[
            pltpu.VMEM((GROUP_ROWS + 2 * HALO, CH), bf16),
            pltpu.VMEM((GROUP_ROWS + 2 * HALO, CH), f32),
            pltpu.VMEM((ROUNDS, FLAG_ROWS + GROUP_ROWS, CH), bf16),
            pltpu.VMEM((GROUP // 2, 2 * CH, CH), bf16),
            pltpu.VMEM((ROUNDS, HALF, CH), f32),
            pltpu.VMEM((HALF * STRIDE, CH), f32),
            pltpu.VMEM((ROUNDS, LAG_STORE * HALF, CH), f32),
            pltpu.VMEM((ROUNDS, 3, LAGS * OWN_ROWS, CH), bf16),
            pltpu.VMEM((ROUNDS, 3, LAGS * OWN_ROWS, CH), bf16),
            dma, dma((len(ACROSS),)), dma((len(ACROSS),)), dma((2,)), dma((2,)), dma((3,)), dma((3,)),
            dma((3, PIECES)), dma((3, PIECES)), dma((ROUNDS, 6)), dma((ROUNDS, 6)),
        ],
        compiler_params=pltpu.CompilerParams(
            collective_id=0, has_side_effects=True, vmem_limit_bytes=48 << 20
        ),
        name="correlate",
    )(raw, flags, make_table())
    return out.reshape(ROUNDS, 1, LAGS, OWN_ROWS, CH)


def solution(mesh):
    return jax.shard_map(
        on_device,
        mesh=mesh,
        in_specs=(P(None, "freq", None, "chan"), P(None, "chan")),
        out_specs=P(None, "chan", None, "freq", None),
        check_vma=False,
    )
```

time: 127 us -> 104 us (0.82)
  the two profiles are of different devices: /device:TPU:3 before, /device:TPU:33 now
where the time goes in v2:
time: 104 us; the launch traced here: 103 us
  Pallas kernels  98.6 us (95%)
  local copies, waits for them, and re-layouts  3.26 us (3%)
    pallas_call x1, Pallas kernels, on_device(): pl.pallas_call(kernel, out_shape=jax.ShapeDtypeStruct((ROUNDS, LAGS * OWN...  98.6 us

profile of v2, /device:TPU:33, one launch (start us, length us, event | category | flops | bytes accessed | tf_op | source)
XLA Modules:
  0.0 102.6 jit_solution(8243771478836617151)
XLA Ops:
  0.0 0.7 convert_element_type.5
  0.7 1.2 %copy.4 = bf16[5,4,34,2,128]{4,1,3,0,2:T(4,128)(2,1)S(1)} copy(bf16[5,4,34,2,128]{4,3,2,1,0:T(2,128)(2,1)} %bitcast.10) | data formatting | bytes 696320 | tf_op jit(solution)/shard_map/reshape | solution.py:407
  1.9 0.0 copy-start
  1.9 0.9 copy-done
  2.8 98.6 %correlate.1 = f32[4,816,128]{2,1,0:T(8,128)S(1)} custom-call(bf16[1360,128]{1,0:T(8,128)(2,1)S(1)} %bitcast.9, f32[48,128]{1,0:T(8,128)S(1)} %pad.4.flags, bf16[4,64,136]{2,1,0:T(8,128)(2,1)S(1)} %copy-done), custom_call_target="tpu_custom_call" | custom-call | tf_op jit(solution)/shard_map/correlate/pallas_call | solution.py:415
  101.4 1.2 %copy.7 = f32[4,1,51,16,128]{4,3,2,1,0:T(8,128)} copy(f32[4,1,51,16,128]{4,3,2,1,0:T(8,128)S(1)} %bitcast.8) | data formatting | bytes 3342336
  (3 shorter events, 0.0 us)
Async XLA Ops:
  1.9 0.9 copy-start

commit v3 on v2

--- a/solution.py
+++ b/solution.py
@@ -65,9 +65,9 @@
 
 
 def kernel(
-    raw, flags, table, out,
-    band, mag, white, lhs, inverse, spread, lagged, outbox, inbox,
-    load_sem, z_send, z_recv, h_send, h_recv, f_send, f_recv, x_send, x_recv, y_send, y_recv,
+    raw, usable, tables, out,
+    band, mag, white, lhs, inverse, spread, lagged, outbox, inbox, detour, flags_in, flags, table,
+    load_sem, z_send, z_recv, h_send, h_recv, f_send, f_recv, x_send, x_recv, w_send, w_recv, y_send, y_recv,
 ):
     i, j = lax.axis_index("chan"), lax.axis_index("freq")
     y, zhi = j // 2, j % 2
@@ -95,15 +95,27 @@
             device_id=device, device_id_type=MESH,
         )
 
-    load = pltpu.make_async_copy(raw, band.at[pl.ds(HALO + zhi * BAND_ROWS, BAND_ROWS)], load_sem)
-    load.start()
+    loads = [
+        pltpu.make_async_copy(usable, flags_in, load_sem.at[0]),
+        pltpu.make_async_copy(raw, band.at[pl.ds(HALO + zhi * BAND_ROWS, BAND_ROWS)], load_sem.at[1]),
+        pltpu.make_async_copy(tables.at[y], table, load_sem.at[2]),
+    ]
+    for load in loads:
+        load.start()
     barrier = pltpu.get_barrier_semaphore()
     partners = [across] + [along_y(d) for d in (1, 3)]
-    partners += [ahead(r) for r in (1, 2, 3, -1, -2, -3)]
+    partners += [ahead(r) for r in (1, 2, 3, 4, -1, -2, -3, -4)]
     for partner in partners:
         pl.semaphore_signal(barrier, inc=1, device_id=partner, device_id_type=MESH)
+    loads[0].wait()
+    once = flags_in[...].astype(jnp.float32)
+    for g in range(5):
+        flags[8 * g : 8 * g + 4, :] = once[4 * g : 4 * g + 4, :]
+        flags[8 * g + 4 : 8 * g + 8, :] = once[4 * g : 4 * g + 4, :]
+    flags[ROWS:FLAG_ROWS, :] = jnp.zeros((FLAG_ROWS - ROWS, CH), jnp.float32)
     white[0, 0:FLAG_ROWS, :] = flags[...].astype(jnp.bfloat16)
-    load.wait()
+    for load in loads[1:]:
+        load.wait()
     pl.semaphore_wait(barrier, len(partners))
 
     def z_copy(k):
@@ -203,11 +215,11 @@
         for g in range(4):
             inverse[r, g * 16 : (g + 1) * 16, :] = scale[g * 32 : g * 32 + 16, :]
 
-    def lag_sums(r):
-        tab = table[y]
+    def lag_sums(r, to):
+        tab = table[...]
 
         def body(p):
-            a = 2 * p
+            a = OWN_ROWS * to + 2 * p
             s0 = spread[pl.ds(pl.multiple_of(a * STRIDE, 8), STRIDE), :].astype(jnp.bfloat16)
             s1 = spread[pl.ds(pl.multiple_of((a + 1) * STRIDE, 8), STRIDE), :].astype(jnp.bfloat16)
             both = jnp.concatenate([s0, s1], axis=1)
@@ -215,7 +227,7 @@
             lagged[r, pl.ds(a, LAG_STORE, stride=HALF), :] = c[0:LAG_STORE, 0:CH]
             lagged[r, pl.ds(a + 1, LAG_STORE, stride=HALF), :] = c[0:LAG_STORE, CH : 2 * CH]
 
-        loop(HALF // 2, body)
+        loop(OWN_ROWS // 2, body)
 
     PARTS = ((2, 0, 1), (2, CUT, 3), (1, CUT, 1), (3, 0, 3), (1, 0, 1), (3, CUT, 3))
 
@@ -241,10 +253,15 @@
         loop((CUT if row == 0 else FULL - CUT) // OWN_ROWS, body)
 
     def lags(r):
-        lag_sums(r)
-        for n in range(4):
+        lag_sums(r, (y + 2) % 4)
+        for n in (0, 1):
             pack_round(r, n)
             y_copy(r, n).start()
+        for n in (2, 3):
+            lag_sums(r, (y + PARTS[n][0]) % 4)
+            pack_round(r, n)
+            y_copy(r, n).start()
+        lag_sums(r, y)
 
     def relay(r):
         for n in (0, 1):
@@ -285,9 +302,28 @@
     def pass_on(k):
         return remote(piece(2, k, before), piece(3, k, before), x_send.at[0, k], x_recv.at[2, k], ahead(1))
 
+    def detour_rows(k):
+        first, pairs = WHITEN[k]
+        return detour.at[pl.ds(first_pair(first, pairs, zhi) * PAIR, pairs * PAIR)]
+
+    def detour_in(k):
+        return remote(piece(0, k, zhi), detour_rows(k), w_send.at[k], w_recv.at[k], ahead(-2))
+
+    def detour_out(k):
+        return remote(detour_rows(k), piece(2, k, zhi), w_send.at[k], x_recv.at[1, k], ahead(4))
+
+    last_odd = (x_index == 3) & (core == 1)
+    last_even = (x_index == 3) & (core == 0)
+    helper = (x_index == 2) & (core == 1)
+
     def send_own(k):
         pl.when(core == 0)(to_sibling(k).start)
         pl.when(x_index != 3)(to_next(k).start)
+        pl.when(last_odd)(detour_in(k).start)
+
+    def help_out(k):
+        detour_in(k).wait_recv()
+        detour_out(k).start()
 
     def forward(k):
         to_next(k).wait_recv()
@@ -311,15 +347,13 @@
 
     def receive_across(k):
         z_copy(k).wait_recv()
-        if k + 2 < len(ACROSS):
-            z_copy(k + 2).start()
         if k == 0:
             send_halo(0)
         first, pairs = ACROSS[k]
         magnitudes(HALO + first_pair(first, pairs, 1 - zhi) * PAIR, pairs)
 
-    z_copy(0).start()
-    z_copy(1).start()
+    for k in range(len(ACROSS)):
+        z_copy(k).start()
     send_halo(1)
     for copy in flag_copies:
         copy.start()
@@ -354,39 +388,57 @@
                 flag_copies[r - 1].wait_recv()
                 usable_pairs(r)
 
-    @pl.when(x_index == 3)
+    @pl.when(last_even)
     def _():
         for k in range(PIECES):
             to_next(k).start()
 
+    @pl.when(helper)
+    def _():
+        for k in range(PIECES - 1):
+            help_out(k)
+
     forward_early(PIECES - 2)
     cross_piece(PIECES - 1)
     lags(0)
+    pl.when(helper)(lambda: help_out(PIECES - 1))
     forward_early(PIECES - 1)
 
-    @pl.when((x_index == 3) & (core == 1))
+    @pl.when(last_odd)
     def _():
         for k in range(PIECES):
             pass_on(k).start()
 
-    @pl.when(x_index == 0)
-    def _():
+    def forward_late():
         for k in range(PIECES):
             forward(k)
 
-    for r in (1, 2, 3):
-        if r != 2:
-            for k in range(PIECES):
-                remote(
-                    piece(r, k, zhi), piece(r, k, zhi), x_send.at[0, k], x_recv.at[r - 1, k], ahead(1)
-                ).wait_recv()
-        cross(r, 0, PAIRS)
-        lags(r)
-        relay(r - 1)
+    def receive(slot):
+        for k in range(PIECES):
+            remote(
+                piece(slot, k, zhi), piece(slot, k, zhi), x_send.at[0, k], x_recv.at[slot - 1, k], ahead(1)
+            ).wait_recv()
+
+    second, third = 2 - core, 1 + core
+    pl.when((x_index == 0) & (core == 0))(forward_late)
+    pl.when(core == 1)(lambda: receive(1))
+    cross(second, 0, PAIRS)
+    lags(second)
+    relay(0)
+    pl.when((x_index == 0) & (core == 1))(forward_late)
+    pl.when(core == 0)(lambda: receive(1))
+    cross(third, 0, PAIRS)
+    lags(third)
+    relay(second)
+    receive(3)
+    cross(3, 0, PAIRS)
+    lags(3)
+    relay(third)
     finish(0)
+    finish(second)
     relay(3)
-    for r in (1, 2, 3):
-        finish(r)
+    finish(third)
+    finish(3)
 
     for k in range(len(ACROSS)):
         z_copy(k).wait_send()
@@ -395,7 +447,8 @@
     for copy in flag_copies:
         copy.wait_send()
     for k in range(PIECES):
-        to_next(k).wait_send()
+        pl.when(jnp.logical_not(last_odd))(to_next(k).wait_send)
+        pl.when(last_odd | helper)(detour_in(k).wait_send)
         to_sibling(k).wait_send()
         pass_up(k).wait_send()
     for r in range(ROUNDS):
@@ -406,16 +459,13 @@
 def on_device(spectra, valid):
     groups = spectra.reshape(5, 4, BAND, 2, CH)
     raw = jnp.transpose(groups, (2, 0, 3, 1, 4)).reshape(BAND_ROWS, CH)
-    flags = valid.astype(jnp.float32).reshape(5, 1, 4, CH)
-    flags = jnp.broadcast_to(flags, (5, 2, 4, CH)).reshape(ROWS, CH)
-    flags = jnp.pad(flags, ((0, FLAG_ROWS - ROWS), (0, 0)))
     vmem = pl.BlockSpec(memory_space=pltpu.VMEM)
     dma = pltpu.SemaphoreType.DMA
     bf16, f32 = jnp.bfloat16, jnp.float32
     out = pl.pallas_call(
         kernel,
         out_shape=jax.ShapeDtypeStruct((ROUNDS, LAGS * OWN_ROWS, CH), f32),
-        in_specs=[pl.BlockSpec(memory_space=pl.ANY), vmem, vmem],
+        in_specs=[pl.BlockSpec(memory_space=pl.ANY)] * 3,
         out_specs=vmem,
         scratch_shapes=[
             pltpu.VMEM((GROUP_ROWS + 2 * HALO, CH), bf16),
@@ -427,14 +477,18 @@
             pltpu.VMEM((ROUNDS, LAG_STORE * HALF, CH), f32),
             pltpu.VMEM((ROUNDS, 3, LAGS * OWN_ROWS, CH), bf16),
             pltpu.VMEM((ROUNDS, 3, LAGS * OWN_ROWS, CH), bf16),
-            dma, dma((len(ACROSS),)), dma((len(ACROSS),)), dma((2,)), dma((2,)), dma((3,)), dma((3,)),
-            dma((3, PIECES)), dma((3, PIECES)), dma((ROUNDS, 6)), dma((ROUNDS, 6)),
+            pltpu.VMEM((GROUP_ROWS, CH), bf16),
+            pltpu.VMEM((W, CH), jnp.int32),
+            pltpu.VMEM((FLAG_ROWS, CH), f32),
+            pltpu.VMEM((LAG_PAD, STRIDE), bf16),
+            dma((3,)), dma((len(ACROSS),)), dma((len(ACROSS),)), dma((2,)), dma((2,)), dma((3,)), dma((3,)),
+            dma((3, PIECES)), dma((3, PIECES)), dma((PIECES,)), dma((PIECES,)), dma((ROUNDS, 6)), dma((ROUNDS, 6)),
         ],
         compiler_params=pltpu.CompilerParams(
             collective_id=0, has_side_effects=True, vmem_limit_bytes=48 << 20
         ),
         name="correlate",
-    )(raw, flags, make_table())
+    )(raw, valid, make_table())
     return out.reshape(ROUNDS, 1, LAGS, OWN_ROWS, CH)
 
 

time: 104 us -> 98.4 us (0.946)
  the two profiles are of different devices: /device:TPU:33 before, /device:TPU:8 now
where the time goes in v3:
time: 98.4 us; the launch traced here: 98.1 us
  Pallas kernels  94.2 us (96%)
  local copies, waits for them, and re-layouts  3.94 us (4%)
    pallas_call x1, Pallas kernels, on_device(): pl.pallas_call(kernel, out_shape=jax.ShapeDtypeStruct((ROUNDS, LAGS * OWN...  94.2 us
    unnamed x5, local copies, waits for them, and re-layouts  2.78 us

profile of v3, /device:TPU:8, one launch (start us, length us, event | category | flops | bytes accessed | tf_op | source)
XLA Modules:
  0.0 98.1 jit_solution(7733503223471430416)
XLA Ops:
  0.0 1.2 %copy.4 = bf16[5,4,34,2,128]{4,1,3,0,2:T(4,128)(2,1)S(1)} copy(bf16[5,4,34,2,128]{4,3,2,1,0:T(2,128)(2,1)} %bitcast.9) | data formatting | bytes 696320 | tf_op jit(solution)/shard_map/reshape | solution.py:460
  1.2 0.0 copy-start
  1.2 0.9 copy-done
  2.1 0.0 copy-start.1
  2.1 0.7 copy-done.1
  2.8 94.2 %correlate.1 = f32[4,816,128]{2,1,0:T(8,128)S(1)} custom-call(bf16[1360,128]{1,0:T(8,128)(2,1)S(1)} %bitcast.8, s32[20,128]{1,0:T(8,128)S(1)} %copy-done.1, bf16[4,64,136]{2,1,0:T(8,128)(2,1)S(1)} %copy-done), custom_call_target="tpu_custom_call" | custom-call | tf_op jit(solution)/shard_map/correlate/pallas_call | solution.py:465
  97.0 1.2 %copy.7 = f32[4,1,51,16,128]{4,3,2,1,0:T(8,128)} copy(f32[4,1,51,16,128]{4,3,2,1,0:T(8,128)S(1)} %bitcast.7) | data formatting | bytes 3342336
Async XLA Ops:
  1.2 0.9 copy-start
  2.1 0.7 copy-start.1

commit v4 on v3

--- a/solution.py
+++ b/solution.py
@@ -2,7 +2,6 @@
 
 import jax
 import jax.numpy as jnp
-import numpy as np
 from jax import lax
 from jax.experimental import pallas as pl
 from jax.experimental.pallas import tpu as pltpu
@@ -35,6 +34,8 @@
 ACROSS = ((0, 2), (12, 5), (8, 4), (4, 4), (2, 2))
 WHITEN = ((2, 13), (0, 2), (15, 5), (20, 4), (24, 4), (28, 6))
 PIECES = len(WHITEN)
+EVEN_BY = (0, 1, 1, 1, 2, 2)
+TURN = 1
 
 water_level = 0.5
 first_bin = 30.0
@@ -42,16 +43,6 @@
 MESH = pl.DeviceIdType.MESH
 
 
-def make_table():
-    lag_index = np.arange(LAGS, dtype=np.float32) - np.float32(LAGS // 2)
-    bin_freq = np.float32(first_bin) + np.arange(BINS, dtype=np.float32)
-    phase = np.float32(2.0 * math.pi) * lag_index[:, None] * bin_freq[None, :] / np.float32(period)
-    both = np.stack([np.cos(phase), -np.sin(phase)], axis=1).reshape(LAGS, 2, 4, GROUP)
-    table = np.zeros((4, LAG_PAD, 2, GROUP), np.float32)
-    table[:, :LAGS] = both.transpose(2, 0, 1, 3)
-    return jnp.asarray(table.reshape(4, LAG_PAD, STRIDE), jnp.bfloat16)
-
-
 def roll4(x):
     return pltpu.roll(x, 4, axis=1)
 
@@ -65,9 +56,9 @@
 
 
 def kernel(
-    raw, usable, tables, out,
+    raw, usable, out,
     band, mag, white, lhs, inverse, spread, lagged, outbox, inbox, detour, flags_in, flags, table,
-    load_sem, z_send, z_recv, h_send, h_recv, f_send, f_recv, x_send, x_recv, w_send, w_recv, y_send, y_recv,
+    load_sem, go_sem, z_send, z_recv, h_send, h_recv, f_send, f_recv, x_send, x_recv, w_send, w_recv, y_send, y_recv,
 ):
     i, j = lax.axis_index("chan"), lax.axis_index("freq")
     y, zhi = j // 2, j % 2
@@ -85,6 +76,7 @@
         return {"chan": i, "freq": ((y + d) % 4) * 2 + zhi}
 
     across = {"chan": i, "freq": j + 1 - 2 * zhi}
+    sibling = {"chan": i + 1 - 2 * core, "freq": j}
 
     def first_pair(first, pairs, origin):
         return first + origin * (PAIRS - 2 * first - pairs)
@@ -98,13 +90,12 @@
     loads = [
         pltpu.make_async_copy(usable, flags_in, load_sem.at[0]),
         pltpu.make_async_copy(raw, band.at[pl.ds(HALO + zhi * BAND_ROWS, BAND_ROWS)], load_sem.at[1]),
-        pltpu.make_async_copy(tables.at[y], table, load_sem.at[2]),
     ]
     for load in loads:
         load.start()
     barrier = pltpu.get_barrier_semaphore()
     partners = [across] + [along_y(d) for d in (1, 3)]
-    partners += [ahead(r) for r in (1, 2, 3, 4, -1, -2, -3, -4)]
+    partners += [ahead(r) for r in (1, 2, 3, 4, 6, -1, -2, -3, -4, -6)]
     for partner in partners:
         pl.semaphore_signal(barrier, inc=1, device_id=partner, device_id_type=MESH)
     loads[0].wait()
@@ -149,6 +140,16 @@
     sign = jnp.where(sublane < 4, -1.0, 1.0)
     first_half = (lane % 32) < 16
     valid = flags[0:ROWS, :]
+
+    def make_table():
+        lag = lax.broadcasted_iota(jnp.int32, (LAG_PAD, STRIDE), 0)
+        column = lax.broadcasted_iota(jnp.int32, (LAG_PAD, STRIDE), 1)
+        bins = y * GROUP + jnp.where(column < GROUP, column, column - GROUP)
+        lag_index = lag.astype(jnp.float32) - float(LAGS // 2)
+        bin_freq = first_bin + bins.astype(jnp.float32)
+        phase_angle = 2.0 * math.pi * lag_index * bin_freq / period
+        both = jnp.where(column < GROUP, jnp.cos(phase_angle), -jnp.sin(phase_angle))
+        table[...] = jnp.where(lag < LAGS, both, 0.0).astype(jnp.bfloat16)
 
     def magnitudes(row, pairs):
         def body(p):
@@ -307,23 +308,49 @@
         return detour.at[pl.ds(first_pair(first, pairs, zhi) * PAIR, pairs * PAIR)]
 
     def detour_in(k):
-        return remote(piece(0, k, zhi), detour_rows(k), w_send.at[k], w_recv.at[k], ahead(-2))
+        return remote(piece(0, k, zhi), detour_rows(k), w_send.at[k], w_recv.at[k], ahead(-4))
 
     def detour_out(k):
-        return remote(detour_rows(k), piece(2, k, zhi), w_send.at[k], x_recv.at[1, k], ahead(4))
+        return remote(detour_rows(k), piece(2, k, zhi), w_send.at[k], x_recv.at[1, k], ahead(6))
+
+    def jump(k):
+        return remote(piece(0, k, zhi), piece(3, k, zhi), w_send.at[k], x_recv.at[2, k], ahead(3))
+
+    def detour_even(k):
+        chips = EVEN_BY[k]
+        return remote(piece(0, k, zhi), detour_rows(k), w_send.at[k], w_recv.at[k], ahead(-2 * chips))
+
+    def detour_even_out(k):
+        chips = EVEN_BY[k]
+        return remote(detour_rows(k), piece(2, k, zhi), w_send.at[k], x_recv.at[1, k], ahead(2 + 2 * chips))
+
+    def even_helper(k):
+        return (x_index == 3 - EVEN_BY[k]) & (core == 0)
+
+    def help_even(k):
+        if EVEN_BY[k]:
+            @pl.when(even_helper(k))
+            def _():
+                detour_even(k).wait_recv()
+                detour_even_out(k).start()
 
     last_odd = (x_index == 3) & (core == 1)
     last_even = (x_index == 3) & (core == 0)
-    helper = (x_index == 2) & (core == 1)
+    jumper = (x_index == 2) & (core == 1)
+    helper = (x_index == 1) & (core == 1)
 
     def send_own(k):
         pl.when(core == 0)(to_sibling(k).start)
         pl.when(x_index != 3)(to_next(k).start)
+        pl.when(last_even)(detour_even(k).start if EVEN_BY[k] else to_next(k).start)
         pl.when(last_odd)(detour_in(k).start)
 
     def help_out(k):
         detour_in(k).wait_recv()
         detour_out(k).start()
+
+    def go_on():
+        pl.semaphore_signal(go_sem, inc=1, device_id=sibling, device_id_type=MESH)
 
     def forward(k):
         to_next(k).wait_recv()
@@ -352,13 +379,19 @@
         first, pairs = ACROSS[k]
         magnitudes(HALO + first_pair(first, pairs, 1 - zhi) * PAIR, pairs)
 
-    for k in range(len(ACROSS)):
-        z_copy(k).start()
+    z_copy(0).start()
+
+    @pl.when(core == 0)
+    def _():
+        for k in range(1, len(ACROSS)):
+            z_copy(k).start()
+
     send_halo(1)
     for copy in flag_copies:
         copy.start()
     magnitudes(HALO + zhi * BAND_ROWS, BAND // 2)
     whiten_piece(0)
+    make_table()
     usable_pairs(0)
     receive_across(0)
     cross_piece(0)
@@ -377,10 +410,20 @@
 
     whiten_piece(1)
     cross_piece(1)
+
+    @pl.when(core == 1)
+    def _():
+        pl.semaphore_wait(go_sem, 1)
+        for k in range(1, len(ACROSS)):
+            z_copy(k).start()
+
     for k in range(2, PIECES):
         receive_across(k - 1)
+        if k - 1 == TURN:
+            pl.when(core == 0)(go_on)
         whiten_piece(k)
         forward_early(k - 2)
+        help_even(k - 2)
         if k < PIECES - 1:
             cross_piece(k)
         if k == 3:
@@ -388,10 +431,10 @@
                 flag_copies[r - 1].wait_recv()
                 usable_pairs(r)
 
-    @pl.when(last_even)
+    @pl.when(jumper)
     def _():
         for k in range(PIECES):
-            to_next(k).start()
+            jump(k).start()
 
     @pl.when(helper)
     def _():
@@ -399,15 +442,13 @@
             help_out(k)
 
     forward_early(PIECES - 2)
+    help_even(PIECES - 2)
     cross_piece(PIECES - 1)
     lags(0)
     pl.when(helper)(lambda: help_out(PIECES - 1))
     forward_early(PIECES - 1)
-
-    @pl.when(last_odd)
-    def _():
-        for k in range(PIECES):
-            pass_on(k).start()
+    help_even(PIECES - 1)
+    pl.when(core == 0)(lambda: relay(0))
 
     def forward_late():
         for k in range(PIECES):
@@ -419,26 +460,31 @@
                 piece(slot, k, zhi), piece(slot, k, zhi), x_send.at[0, k], x_recv.at[slot - 1, k], ahead(1)
             ).wait_recv()
 
-    second, third = 2 - core, 1 + core
-    pl.when((x_index == 0) & (core == 0))(forward_late)
+    first_chip = x_index == 0
+    second = 2 - core
+    third = jnp.where(first_chip, 3, 1 + core)
+    fourth = jnp.where(first_chip, 1 + core, 3)
+    pl.when(first_chip & (core == 0))(forward_late)
     pl.when(core == 1)(lambda: receive(1))
     cross(second, 0, PAIRS)
     lags(second)
-    relay(0)
-    pl.when((x_index == 0) & (core == 1))(forward_late)
-    pl.when(core == 0)(lambda: receive(1))
+    relay(jnp.where(core == 0, second, 0))
+    pl.when(first_chip)(lambda: receive(3))
+    pl.when(jnp.logical_not(first_chip) & (core == 0))(lambda: receive(1))
     cross(third, 0, PAIRS)
     lags(third)
-    relay(second)
-    receive(3)
-    cross(3, 0, PAIRS)
-    lags(3)
+    pl.when(core == 1)(lambda: relay(1))
+    pl.when(first_chip & (core == 1))(forward_late)
+    pl.when(first_chip & (core == 0))(lambda: receive(1))
+    pl.when(jnp.logical_not(first_chip))(lambda: receive(3))
+    cross(fourth, 0, PAIRS)
+    lags(fourth)
     relay(third)
     finish(0)
     finish(second)
-    relay(3)
+    relay(fourth)
     finish(third)
-    finish(3)
+    finish(fourth)
 
     for k in range(len(ACROSS)):
         z_copy(k).wait_send()
@@ -447,9 +493,11 @@
     for copy in flag_copies:
         copy.wait_send()
     for k in range(PIECES):
-        pl.when(jnp.logical_not(last_odd))(to_next(k).wait_send)
-        pl.when(last_odd | helper)(detour_in(k).wait_send)
-        to_sibling(k).wait_send()
+        detoured = last_odd | last_even if EVEN_BY[k] else last_odd
+        helping = helper | even_helper(k) if EVEN_BY[k] else helper
+        pl.when(jnp.logical_not(detoured))(to_next(k).wait_send)
+        pl.when(detoured | helping | jumper)(detour_in(k).wait_send)
+        pl.when(jnp.logical_not(last_odd))(to_sibling(k).wait_send)
         pass_up(k).wait_send()
     for r in range(ROUNDS):
         for n in range(len(PARTS)):
@@ -459,14 +507,13 @@
 def on_device(spectra, valid):
     groups = spectra.reshape(5, 4, BAND, 2, CH)
     raw = jnp.transpose(groups, (2, 0, 3, 1, 4)).reshape(BAND_ROWS, CH)
-    vmem = pl.BlockSpec(memory_space=pltpu.VMEM)
     dma = pltpu.SemaphoreType.DMA
     bf16, f32 = jnp.bfloat16, jnp.float32
     out = pl.pallas_call(
         kernel,
         out_shape=jax.ShapeDtypeStruct((ROUNDS, LAGS * OWN_ROWS, CH), f32),
-        in_specs=[pl.BlockSpec(memory_space=pl.ANY)] * 3,
-        out_specs=vmem,
+        in_specs=[pl.BlockSpec(memory_space=pl.ANY)] * 2,
+        out_specs=pl.BlockSpec(memory_space=pltpu.VMEM),
         scratch_shapes=[
             pltpu.VMEM((GROUP_ROWS + 2 * HALO, CH), bf16),
             pltpu.VMEM((GROUP_ROWS + 2 * HALO, CH), f32),
@@ -481,14 +528,14 @@
             pltpu.VMEM((W, CH), jnp.int32),
             pltpu.VMEM((FLAG_ROWS, CH), f32),
             pltpu.VMEM((LAG_PAD, STRIDE), bf16),
-            dma((3,)), dma((len(ACROSS),)), dma((len(ACROSS),)), dma((2,)), dma((2,)), dma((3,)), dma((3,)),
+            dma((2,)), pltpu.SemaphoreType.REGULAR, dma((len(ACROSS),)), dma((len(ACROSS),)), dma((2,)), dma((2,)), dma((3,)), dma((3,)),
             dma((3, PIECES)), dma((3, PIECES)), dma((PIECES,)), dma((PIECES,)), dma((ROUNDS, 6)), dma((ROUNDS, 6)),
         ],
         compiler_params=pltpu.CompilerParams(
             collective_id=0, has_side_effects=True, vmem_limit_bytes=48 << 20
         ),
         name="correlate",
-    )(raw, valid, make_table())
+    )(raw, valid)
     return out.reshape(ROUNDS, 1, LAGS, OWN_ROWS, CH)
 
 

time: 98.4 us -> 93.7 us (0.952)
  the two profiles are of different devices: /device:TPU:8 before, /device:TPU:7 now
where the time goes in v4:
time: 93.7 us; the launch traced here: 93.5 us
  Pallas kernels  90.4 us (96%)
  local copies, waits for them, and re-layouts  3.04 us (3%)
    pallas_call x1, Pallas kernels, on_device(): pl.pallas_call(kernel, out_shape=jax.ShapeDtypeStruct((ROUNDS, LAGS * OWN...  90.4 us
    unnamed x3, local copies, waits for them, and re-layouts  1.88 us

profile of v4, /device:TPU:7, one launch (start us, length us, event | category | flops | bytes accessed | tf_op | source)
XLA Modules:
  0.0 93.5 jit_solution(4879569970607650999)
XLA Ops:
  0.0 1.2 %copy.3 = bf16[5,4,34,2,128]{4,1,3,0,2:T(4,128)(2,1)S(1)} copy(bf16[5,4,34,2,128]{4,3,2,1,0:T(2,128)(2,1)} %bitcast.9) | data formatting | bytes 696320 | tf_op jit(solution)/shard_map/reshape | solution.py:508
  1.2 0.0 copy-start
  1.2 0.7 copy-done
  1.9 90.4 %correlate.1 = f32[4,816,128]{2,1,0:T(8,128)S(1)} custom-call(bf16[1360,128]{1,0:T(8,128)(2,1)S(1)} %bitcast.8, s32[20,128]{1,0:T(8,128)S(1)} %copy-done), custom_call_target="tpu_custom_call" | custom-call | tf_op jit(solution)/shard_map/correlate/pallas_call | solution.py:512
  92.3 1.2 %copy.6 = f32[4,1,51,16,128]{4,3,2,1,0:T(8,128)} copy(f32[4,1,51,16,128]{4,3,2,1,0:T(8,128)S(1)} %bitcast.7) | data formatting | bytes 3342336
Async XLA Ops:
  1.2 0.7 copy-start

commit v5 on v4

--- a/solution.py
+++ b/solution.py
@@ -1,3 +1,4 @@
+import functools
 import math
 
 import jax
@@ -34,7 +35,7 @@
 ACROSS = ((0, 2), (12, 5), (8, 4), (4, 4), (2, 2))
 WHITEN = ((2, 13), (0, 2), (15, 5), (20, 4), (24, 4), (28, 6))
 PIECES = len(WHITEN)
-EVEN_BY = (0, 1, 1, 1, 2, 2)
+LEFT = ((0, 2, 2, 2, 3, 3), (1, 2, 2, 3, 2, 3))
 TURN = 1
 
 water_level = 0.5
@@ -95,7 +96,7 @@
         load.start()
     barrier = pltpu.get_barrier_semaphore()
     partners = [across] + [along_y(d) for d in (1, 3)]
-    partners += [ahead(r) for r in (1, 2, 3, 4, 6, -1, -2, -3, -4, -6)]
+    partners += [ahead(r) for r in (1, 2, 3, 4, 6, 8, -1, -2, -3, -4, -6, -8)]
     for partner in partners:
         pl.semaphore_signal(barrier, inc=1, device_id=partner, device_id_type=MESH)
     loads[0].wait()
@@ -307,47 +308,31 @@
         first, pairs = WHITEN[k]
         return detour.at[pl.ds(first_pair(first, pairs, zhi) * PAIR, pairs * PAIR)]
 
-    def detour_in(k):
-        return remote(piece(0, k, zhi), detour_rows(k), w_send.at[k], w_recv.at[k], ahead(-4))
-
-    def detour_out(k):
-        return remote(detour_rows(k), piece(2, k, zhi), w_send.at[k], x_recv.at[1, k], ahead(6))
-
-    def jump(k):
-        return remote(piece(0, k, zhi), piece(3, k, zhi), w_send.at[k], x_recv.at[2, k], ahead(3))
-
-    def detour_even(k):
-        chips = EVEN_BY[k]
+    def detour_in(k, chips):
         return remote(piece(0, k, zhi), detour_rows(k), w_send.at[k], w_recv.at[k], ahead(-2 * chips))
 
-    def detour_even_out(k):
-        chips = EVEN_BY[k]
+    def detour_out(k, chips):
         return remote(detour_rows(k), piece(2, k, zhi), w_send.at[k], x_recv.at[1, k], ahead(2 + 2 * chips))
 
-    def even_helper(k):
-        return (x_index == 3 - EVEN_BY[k]) & (core == 0)
-
-    def help_even(k):
-        if EVEN_BY[k]:
-            @pl.when(even_helper(k))
+    last_chip = x_index == 3
+    last_odd = last_chip & (core == 1)
+
+    def helping(side, k):
+        return (core == side) & (x_index == 3 - LEFT[side][k]) & (x_index != 3)
+
+    def help_out(side, k):
+        if LEFT[side][k]:
+            @pl.when(helping(side, k))
             def _():
-                detour_even(k).wait_recv()
-                detour_even_out(k).start()
-
-    last_odd = (x_index == 3) & (core == 1)
-    last_even = (x_index == 3) & (core == 0)
-    jumper = (x_index == 2) & (core == 1)
-    helper = (x_index == 1) & (core == 1)
+                detour_in(k, LEFT[side][k]).wait_recv()
+                detour_out(k, LEFT[side][k]).start()
 
     def send_own(k):
         pl.when(core == 0)(to_sibling(k).start)
         pl.when(x_index != 3)(to_next(k).start)
-        pl.when(last_even)(detour_even(k).start if EVEN_BY[k] else to_next(k).start)
-        pl.when(last_odd)(detour_in(k).start)
-
-    def help_out(k):
-        detour_in(k).wait_recv()
-        detour_out(k).start()
+        for side in (0, 1):
+            chips = LEFT[side][k]
+            pl.when(last_chip & (core == side))(detour_in(k, chips).start if chips else to_next(k).start)
 
     def go_on():
         pl.semaphore_signal(go_sem, inc=1, device_id=sibling, device_id_type=MESH)
@@ -423,7 +408,10 @@
             pl.when(core == 0)(go_on)
         whiten_piece(k)
         forward_early(k - 2)
-        help_even(k - 2)
+        help_out(0, k - 2)
+        help_out(1, k - 2)
+        if k >= 4:
+            pl.when(x_index == 0)(functools.partial(forward, k - 4))
         if k < PIECES - 1:
             cross_piece(k)
         if k == 3:
@@ -431,27 +419,26 @@
                 flag_copies[r - 1].wait_recv()
                 usable_pairs(r)
 
-    @pl.when(jumper)
+    help_out(1, PIECES - 2)
+
+    @pl.when(last_odd)
     def _():
-        for k in range(PIECES):
-            jump(k).start()
-
-    @pl.when(helper)
-    def _():
-        for k in range(PIECES - 1):
-            help_out(k)
+        for k in range(PIECES - 2):
+            pass_on(k).start()
 
     forward_early(PIECES - 2)
-    help_even(PIECES - 2)
+    pl.when(last_odd)(pass_on(PIECES - 2).start)
+    help_out(0, PIECES - 2)
     cross_piece(PIECES - 1)
     lags(0)
-    pl.when(helper)(lambda: help_out(PIECES - 1))
+    help_out(1, PIECES - 1)
     forward_early(PIECES - 1)
-    help_even(PIECES - 1)
+    pl.when(last_odd)(pass_on(PIECES - 1).start)
+    help_out(0, PIECES - 1)
     pl.when(core == 0)(lambda: relay(0))
 
-    def forward_late():
-        for k in range(PIECES):
+    def forward_late(*pieces):
+        for k in pieces:
             forward(k)
 
     def receive(slot):
@@ -464,17 +451,18 @@
     second = 2 - core
     third = jnp.where(first_chip, 3, 1 + core)
     fourth = jnp.where(first_chip, 1 + core, 3)
-    pl.when(first_chip & (core == 0))(forward_late)
+    pl.when(first_chip)(lambda: forward_late(2, 3))
+    pl.when(first_chip & (core == 0))(lambda: forward_late(4, 5))
     pl.when(core == 1)(lambda: receive(1))
     cross(second, 0, PAIRS)
     lags(second)
     relay(jnp.where(core == 0, second, 0))
+    pl.when(first_chip & (core == 1))(lambda: forward_late(4, 5))
     pl.when(first_chip)(lambda: receive(3))
     pl.when(jnp.logical_not(first_chip) & (core == 0))(lambda: receive(1))
     cross(third, 0, PAIRS)
     lags(third)
     pl.when(core == 1)(lambda: relay(1))
-    pl.when(first_chip & (core == 1))(forward_late)
     pl.when(first_chip & (core == 0))(lambda: receive(1))
     pl.when(jnp.logical_not(first_chip))(lambda: receive(3))
     cross(fourth, 0, PAIRS)
@@ -493,11 +481,14 @@
     for copy in flag_copies:
         copy.wait_send()
     for k in range(PIECES):
-        detoured = last_odd | last_even if EVEN_BY[k] else last_odd
-        helping = helper | even_helper(k) if EVEN_BY[k] else helper
+        detoured, helper = last_chip & (core == 2), core == 2
+        for side in (0, 1):
+            if LEFT[side][k]:
+                detoured = detoured | (last_chip & (core == side))
+                helper = helper | helping(side, k)
         pl.when(jnp.logical_not(detoured))(to_next(k).wait_send)
-        pl.when(detoured | helping | jumper)(detour_in(k).wait_send)
-        pl.when(jnp.logical_not(last_odd))(to_sibling(k).wait_send)
+        pl.when(detoured | helper)(detour_in(k, 2).wait_send)
+        to_sibling(k).wait_send()
         pass_up(k).wait_send()
     for r in range(ROUNDS):
         for n in range(len(PARTS)):

time: 93.7 us -> 91.6 us (0.978)
  the two profiles are of different devices: /device:TPU:7 before, /device:TPU:1 now
where the time goes in v5:
time: 91.6 us; the launch traced here: 91.4 us
  Pallas kernels  88.4 us (97%)
  local copies, waits for them, and re-layouts  3.04 us (3%)
    pallas_call x1, Pallas kernels, on_device(): pl.pallas_call(kernel, out_shape=jax.ShapeDtypeStruct((ROUNDS, LAGS * OWN...  88.4 us
    unnamed x3, local copies, waits for them, and re-layouts  1.88 us

profile of v5, /device:TPU:1, one launch (start us, length us, event | category | flops | bytes accessed | tf_op | source)
XLA Modules:
  0.0 91.4 jit_solution(15858549432590097573)
XLA Ops:
  0.0 1.2 %copy.3 = bf16[5,4,34,2,128]{4,1,3,0,2:T(4,128)(2,1)S(1)} copy(bf16[5,4,34,2,128]{4,3,2,1,0:T(2,128)(2,1)} %bitcast.9) | data formatting | bytes 696320 | tf_op jit(solution)/shard_map/reshape | solution.py:499
  1.2 0.0 copy-start
  1.2 0.7 copy-done
  1.9 88.4 %correlate.1 = f32[4,816,128]{2,1,0:T(8,128)S(1)} custom-call(bf16[1360,128]{1,0:T(8,128)(2,1)S(1)} %bitcast.8, s32[20,128]{1,0:T(8,128)S(1)} %copy-done), custom_call_target="tpu_custom_call" | custom-call | tf_op jit(solution)/shard_map/correlate/pallas_call | solution.py:503
  90.2 1.2 %copy.6 = f32[4,1,51,16,128]{4,3,2,1,0:T(8,128)} copy(f32[4,1,51,16,128]{4,3,2,1,0:T(8,128)S(1)} %bitcast.7) | data formatting | bytes 3342336
Async XLA Ops:
  1.2 0.7 copy-start

commit v6 on v5

--- a/solution.py
+++ b/solution.py
@@ -32,10 +32,10 @@
 HALF = 64
 CUT = 26 * OWN_ROWS
 FULL = LAGS * OWN_ROWS
-ACROSS = ((0, 2), (12, 5), (8, 4), (4, 4), (2, 2))
-WHITEN = ((2, 13), (0, 2), (15, 5), (20, 4), (24, 4), (28, 6))
+ACROSS = ((0, 2), (12, 5), (8, 4), (3, 5), (2, 1))
+WHITEN = ((2, 13), (0, 2), (15, 5), (20, 4), (24, 5), (29, 5))
 PIECES = len(WHITEN)
-LEFT = ((0, 2, 2, 2, 3, 3), (1, 2, 2, 3, 2, 3))
+LEFT = ((0, 2, 1, 2, 3, 0), (1, 2, 2, 3, 1, 0))
 TURN = 1
 
 water_level = 0.5
@@ -99,6 +99,24 @@
     partners += [ahead(r) for r in (1, 2, 3, 4, 6, 8, -1, -2, -3, -4, -6, -8)]
     for partner in partners:
         pl.semaphore_signal(barrier, inc=1, device_id=partner, device_id_type=MESH)
+    pl.semaphore_wait(barrier, len(partners))
+
+    def z_copy(k):
+        first, pairs = ACROSS[k]
+        own = first + zhi * (PAIRS // 2 - 2 * first - pairs)
+        return remote(
+            raw.at[pl.ds(own * PAIR, pairs * PAIR)],
+            band.at[pl.ds(HALO + zhi * BAND_ROWS + own * PAIR, pairs * PAIR)],
+            z_send.at[k], z_recv.at[k], across,
+        )
+
+    z_copy(0).start()
+
+    @pl.when(core == 0)
+    def _():
+        for k in range(1, len(ACROSS)):
+            z_copy(k).start()
+
     loads[0].wait()
     once = flags_in[...].astype(jnp.float32)
     for g in range(5):
@@ -108,12 +126,6 @@
     white[0, 0:FLAG_ROWS, :] = flags[...].astype(jnp.bfloat16)
     for load in loads[1:]:
         load.wait()
-    pl.semaphore_wait(barrier, len(partners))
-
-    def z_copy(k):
-        first, pairs = ACROSS[k]
-        here = band.at[pl.ds(HALO + first_pair(first, pairs, zhi) * PAIR, pairs * PAIR)]
-        return remote(here, here, z_send.at[k], z_recv.at[k], across)
 
     def halo_copy(top):
         src = GROUP_ROWS if top else HALO
@@ -274,9 +286,10 @@
     def total_round(r):
         def body(l):
             at = pl.multiple_of(l * OWN_ROWS, 16)
-            mine = lagged[r, pl.ds(pl.multiple_of(l * HALF + y * OWN_ROWS, 16), OWN_ROWS), :]
-            got = [inbox[r, d, pl.ds(at, OWN_ROWS), :].astype(jnp.float32) for d in (0, 2)]
-            out[r, pl.ds(at, OWN_ROWS), :] = mine + (got[0] + got[1])
+            sums = lagged[r, pl.ds(pl.multiple_of(l * HALF + y * OWN_ROWS, 16), OWN_ROWS), :]
+            for d in (0, 2):
+                sums = sums + inbox[r, d, pl.ds(at, OWN_ROWS), :].astype(jnp.float32)
+            out[r, pl.ds(at, OWN_ROWS), :] = sums
 
         loop(LAGS, body)
 
@@ -363,13 +376,6 @@
             send_halo(0)
         first, pairs = ACROSS[k]
         magnitudes(HALO + first_pair(first, pairs, 1 - zhi) * PAIR, pairs)
-
-    z_copy(0).start()
-
-    @pl.when(core == 0)
-    def _():
-        for k in range(1, len(ACROSS)):
-            z_copy(k).start()
 
     send_halo(1)
     for copy in flag_copies:
@@ -409,9 +415,12 @@
         whiten_piece(k)
         forward_early(k - 2)
         help_out(0, k - 2)
-        help_out(1, k - 2)
-        if k >= 4:
-            pl.when(x_index == 0)(functools.partial(forward, k - 4))
+        if k == 2:
+            help_out(1, 0)
+        if k == 4:
+            pl.when(x_index == 0)(functools.partial(forward, 0))
+        if k == 5:
+            pl.when(last_odd)(pass_on(0).start)
         if k < PIECES - 1:
             cross_piece(k)
         if k == 3:
@@ -419,22 +428,21 @@
                 flag_copies[r - 1].wait_recv()
                 usable_pairs(r)
 
-    help_out(1, PIECES - 2)
+    for k in range(1, PIECES - 2):
+        help_out(1, k)
 
     @pl.when(last_odd)
     def _():
-        for k in range(PIECES - 2):
+        for k in range(1, PIECES - 2):
             pass_on(k).start()
 
-    forward_early(PIECES - 2)
-    pl.when(last_odd)(pass_on(PIECES - 2).start)
-    help_out(0, PIECES - 2)
     cross_piece(PIECES - 1)
     lags(0)
-    help_out(1, PIECES - 1)
-    forward_early(PIECES - 1)
-    pl.when(last_odd)(pass_on(PIECES - 1).start)
-    help_out(0, PIECES - 1)
+    for k in (PIECES - 2, PIECES - 1):
+        forward_early(k)
+        pl.when(last_odd)(pass_on(k).start)
+        help_out(0, k)
+        help_out(1, k)
     pl.when(core == 0)(lambda: relay(0))
 
     def forward_late(*pieces):
@@ -451,17 +459,17 @@
     second = 2 - core
     third = jnp.where(first_chip, 3, 1 + core)
     fourth = jnp.where(first_chip, 1 + core, 3)
-    pl.when(first_chip)(lambda: forward_late(2, 3))
-    pl.when(first_chip & (core == 0))(lambda: forward_late(4, 5))
+    pl.when(first_chip & (core == 0))(lambda: forward_late(1, 2, 3, 4, 5))
     pl.when(core == 1)(lambda: receive(1))
     cross(second, 0, PAIRS)
     lags(second)
+    pl.when(first_chip & (core == 1))(lambda: forward_late(1, 2, 3, 4))
     relay(jnp.where(core == 0, second, 0))
-    pl.when(first_chip & (core == 1))(lambda: forward_late(4, 5))
     pl.when(first_chip)(lambda: receive(3))
     pl.when(jnp.logical_not(first_chip) & (core == 0))(lambda: receive(1))
     cross(third, 0, PAIRS)
     lags(third)
+    pl.when(first_chip & (core == 1))(lambda: forward_late(5))
     pl.when(core == 1)(lambda: relay(1))
     pl.when(first_chip & (core == 0))(lambda: receive(1))
     pl.when(jnp.logical_not(first_chip))(lambda: receive(3))

time: 91.6 us -> 90.3 us (0.986)
  the two profiles are of different devices: /device:TPU:1 before, /device:TPU:33 now
where the time goes in v6:
time: 90.3 us; the launch traced here: 90.1 us
  Pallas kernels  87.1 us (96%)
  local copies, waits for them, and re-layouts  3.04 us (3%)
    pallas_call x1, Pallas kernels, on_device(): pl.pallas_call(kernel, out_shape=jax.ShapeDtypeStruct((ROUNDS, LAGS * OWN...  87.1 us
    unnamed x3, local copies, waits for them, and re-layouts  1.88 us

profile of v6, /device:TPU:33, one launch (start us, length us, event | category | flops | bytes accessed | tf_op | source)
XLA Modules:
  0.0 90.1 jit_solution(11632268894635699193)
XLA Ops:
  0.0 1.2 %copy.3 = bf16[5,4,34,2,128]{4,1,3,0,2:T(4,128)(2,1)S(1)} copy(bf16[5,4,34,2,128]{4,3,2,1,0:T(2,128)(2,1)} %bitcast.9) | data formatting | bytes 696320 | tf_op jit(solution)/shard_map/reshape | solution.py:507
  1.2 0.0 copy-start
  1.2 0.7 copy-done
  1.9 87.1 %correlate.1 = f32[4,816,128]{2,1,0:T(8,128)S(1)} custom-call(bf16[1360,128]{1,0:T(8,128)(2,1)S(1)} %bitcast.8, s32[20,128]{1,0:T(8,128)S(1)} %copy-done), custom_call_target="tpu_custom_call" | custom-call | tf_op jit(solution)/shard_map/correlate/pallas_call | solution.py:511
  89.0 1.2 %copy.6 = f32[4,1,51,16,128]{4,3,2,1,0:T(8,128)} copy(f32[4,1,51,16,128]{4,3,2,1,0:T(8,128)S(1)} %bitcast.7) | data formatting | bytes 3342336
Async XLA Ops:
  1.2 0.7 copy-start

commit v7 on v6

--- a/solution.py
+++ b/solution.py
@@ -519,8 +519,8 @@
             pltpu.VMEM((ROUNDS, FLAG_ROWS + GROUP_ROWS, CH), bf16),
             pltpu.VMEM((GROUP // 2, 2 * CH, CH), bf16),
             pltpu.VMEM((ROUNDS, HALF, CH), f32),
-            pltpu.VMEM((HALF * STRIDE, CH), f32),
-            pltpu.VMEM((ROUNDS, LAG_STORE * HALF, CH), f32),
+            pltpu.VMEM(((HALF + 1) * STRIDE, CH), f32),
+            pltpu.VMEM((ROUNDS, (LAG_STORE + 1) * HALF, CH), f32),
             pltpu.VMEM((ROUNDS, 3, LAGS * OWN_ROWS, CH), bf16),
             pltpu.VMEM((ROUNDS, 3, LAGS * OWN_ROWS, CH), bf16),
             pltpu.VMEM((GROUP_ROWS, CH), bf16),

time: 90.3 us -> 90.3 us (level)
  no operation moved by 1% of the time
where the time goes in v7:
time: 90.3 us; the launch traced here: 90.1 us
  Pallas kernels  87.1 us (96%)
  local copies, waits for them, and re-layouts  3.04 us (3%)
    pallas_call x1, Pallas kernels, on_device(): pl.pallas_call(kernel, out_shape=jax.ShapeDtypeStruct((ROUNDS, LAGS * OWN...  87.1 us
    unnamed x3, local copies, waits for them, and re-layouts  1.88 us

profile of v7, /device:TPU:33, one launch (start us, length us, event | category | flops | bytes accessed | tf_op | source)
XLA Modules:
  0.0 90.1 jit_solution(11960302987440901928)
XLA Ops:
  0.0 1.2 %copy.3 = bf16[5,4,34,2,128]{4,1,3,0,2:T(4,128)(2,1)S(1)} copy(bf16[5,4,34,2,128]{4,3,2,1,0:T(2,128)(2,1)} %bitcast.9) | data formatting | bytes 696320 | tf_op jit(solution)/shard_map/reshape | solution.py:507
  1.2 0.0 copy-start
  1.2 0.7 copy-done
  1.9 87.1 %correlate.1 = f32[4,816,128]{2,1,0:T(8,128)S(1)} custom-call(bf16[1360,128]{1,0:T(8,128)(2,1)S(1)} %bitcast.8, s32[20,128]{1,0:T(8,128)S(1)} %copy-done), custom_call_target="tpu_custom_call" | custom-call | tf_op jit(solution)/shard_map/correlate/pallas_call | solution.py:511
  89.0 1.2 %copy.6 = f32[4,1,51,16,128]{4,3,2,1,0:T(8,128)} copy(f32[4,1,51,16,128]{4,3,2,1,0:T(8,128)S(1)} %bitcast.7) | data formatting | bytes 3342336
Async XLA Ops:
  1.2 0.7 copy-start

commit v8 on v7

--- a/solution.py
+++ b/solution.py
@@ -462,8 +462,9 @@
     pl.when(first_chip & (core == 0))(lambda: forward_late(1, 2, 3, 4, 5))
     pl.when(core == 1)(lambda: receive(1))
     cross(second, 0, PAIRS)
+    pl.when(first_chip & (core == 1))(lambda: forward_late(1, 2, 3))
     lags(second)
-    pl.when(first_chip & (core == 1))(lambda: forward_late(1, 2, 3, 4))
+    pl.when(first_chip & (core == 1))(lambda: forward_late(4))
     relay(jnp.where(core == 0, second, 0))
     pl.when(first_chip)(lambda: receive(3))
     pl.when(jnp.logical_not(first_chip) & (core == 0))(lambda: receive(1))

time: 90.3 us -> 90.3 us (level)
  no operation moved by 1% of the time
where the time goes in v8:
time: 90.3 us; the launch traced here: 90.1 us
  Pallas kernels  87.1 us (96%)
  local copies, waits for them, and re-layouts  3.04 us (3%)
    pallas_call x1, Pallas kernels, on_device(): pl.pallas_call(kernel, out_shape=jax.ShapeDtypeStruct((ROUNDS, LAGS * OWN...  87.1 us
    unnamed x3, local copies, waits for them, and re-layouts  1.88 us

profile of v8, /device:TPU:33, one launch (start us, length us, event | category | flops | bytes accessed | tf_op | source)
XLA Modules:
  0.0 90.1 jit_solution(12330639880407139287)
XLA Ops:
  0.0 1.2 %copy.3 = bf16[5,4,34,2,128]{4,1,3,0,2:T(4,128)(2,1)S(1)} copy(bf16[5,4,34,2,128]{4,3,2,1,0:T(2,128)(2,1)} %bitcast.9) | data formatting | bytes 696320 | tf_op jit(solution)/shard_map/reshape | solution.py:508
  1.2 0.0 copy-start
  1.2 0.7 copy-done
  1.9 87.1 %correlate.1 = f32[4,816,128]{2,1,0:T(8,128)S(1)} custom-call(bf16[1360,128]{1,0:T(8,128)(2,1)S(1)} %bitcast.8, s32[20,128]{1,0:T(8,128)S(1)} %copy-done), custom_call_target="tpu_custom_call" | custom-call | tf_op jit(solution)/shard_map/correlate/pallas_call | solution.py:512
  89.0 1.2 %copy.6 = f32[4,1,51,16,128]{4,3,2,1,0:T(8,128)} copy(f32[4,1,51,16,128]{4,3,2,1,0:T(8,128)S(1)} %bitcast.7) | data formatting | bytes 3342336
Async XLA Ops:
  1.2 0.7 copy-start
